TPU v7x, 512 devices: a whole 4x4x16 slice. The times are simulated.
512 devices in a mesh: rep: 16 (over z_hi, y, core), fsdp: 32 (over z_lo, x).
Axes of the slice: x: 4, y: 4, z: 16 (z_hi: 2, z_lo: 8; z = z_hi * 8 + z_lo), core: 2. Of those that a mesh axis runs over, the one named last changes fastest.
Arguments:
- base_weights: bfloat16 [28672, 832], P('fsdp'), may hold values from -6 to 6
- local_weights: bfloat16 [16, 28672, 832], P('rep', 'fsdp'), may hold values from -6 to 6
- momentum: float32 [28672, 832], P(('fsdp', 'rep')), may hold values from -6 to 6
- sketch_matrix: bfloat16 [28672, 512], P(('fsdp', 'rep')), may hold values from -0.25 to 0.25
Outputs:
- new_weights: bfloat16 [28672, 832], P('fsdp')
- new_momentum: float32 [28672, 832], P(('fsdp', 'rep'))
All inputs are finite; a program needn't handle non-finite values.
Results may differ from a plain program's by a relative error of at most 0.00115.
Values may be sent and summed in bfloat16 or wider, within the bound.
No kernel may reach another device: no remote copies, remote signals or barrier semaphores. Data moves between devices by JAX's collectives and lax.ppermute only.
A program may use at most 64 MiB of HBM per device.

v0:
```python
import jax
import jax.numpy as jnp
from jax import lax
from jax.sharding import PartitionSpec as P


def shards(base_weights, local_weights, momentum, sketch_matrix):
    rows = momentum.shape[0]
    groups = lax.axis_size("rep")
    offset = lax.axis_index("rep") * rows
    base_wide = base_weights.astype(jnp.float32)
    gauss_own = sketch_matrix.astype(jnp.float32)
    drift = base_wide - local_weights[0].astype(jnp.float32)
    partial_sketch = jnp.dot(
        lax.all_gather(sketch_matrix, "rep", axis=0, tiled=True).astype(jnp.float32).T,
        drift,
        precision=lax.Precision.HIGHEST,
        preferred_element_type=jnp.float32,
    )
    sketch = lax.psum(partial_sketch, ("rep", "fsdp")) / groups
    decoded = jnp.dot(
        gauss_own, sketch, precision=lax.Precision.HIGHEST, preferred_element_type=jnp.float32
    )
    new_momentum = 0.9 * momentum + decoded
    base_rows = lax.dynamic_slice_in_dim(base_wide, offset, rows, 0)
    updated = (base_rows - 0.7 * (decoded + 0.9 * new_momentum)).astype(jnp.bfloat16)
    new_weights = lax.all_gather(updated, "rep", axis=0, tiled=True)
    return (new_weights, new_momentum)


def solution(mesh):
    placed = (
        P("fsdp", None),
        P("rep", "fsdp", None),
        P(("fsdp", "rep"), None),
        P(("fsdp", "rep"), None),
    )
    return jax.shard_map(
        shards,
        mesh=mesh,
        in_specs=placed,
        out_specs=(P("fsdp", None), P(("fsdp", "rep"), None)),
        check_vma=False,
    )
```

profile of v0, /device:TPU:1, one launch (start us, length us, event | category | flops | bytes accessed | tf_op | source)
XLA Modules:
  0.0 641.3 jit_solution(15836459508056131185)
XLA Ops:
  7.2 0.0 all-reduce.2.cloned.1.call-start
  7.2 62.8 %all_gather.6 = bf16[896,512]{1,0:T(8,128)(2,1)} all-gather(bf16[56,512]{1,0:T(8,128)(2,1)} %param.7), channel_id=1, replica_groups=mesh['rep'=16,'fsdp'=32] {'rep'}, dimensions={0}, use_global_device_ids=true | all-gather | bytes 974848 | tf_op jit(solution)/shard_map/all_gather | solution.py:15
  70.0 2.9 copy.6
  72.8 2.9 copy.7
  75.7 5.4 fusion.4
  81.1 0.0 all-reduce.2.cloned.1.call-update
  81.1 0.0 all-gather.2.cloned.1.call-start
  81.2 0.0 copy-start
  81.2 0.0 copy-start.1
  81.2 1.9 convert_element_type.14
  83.1 460.3 %all-reduce.2.cloned.1.call-done = f32[512,832]{0,1:T(8,128)} async-done(((f32[512,832]{0,1:T(8,128)}), f32[512,832]{0,1:T(8,128)}) %all-reduce.2.cloned.1.call-update) | async-done | bytes 1703952 | tf_op jit(solution)/shard_map/psum | solution.py:20
  543.4 0.0 copy-done
  543.4 0.0 copy-done.1
  543.4 3.1 subtract_convert_fusion
  546.5 0.0 all-gather.2.cloned.1.call-update
  546.5 84.4 %all-gather.2.cloned.1.call-done = bf16[896,832]{1,0:T(8,128)(2,1)} async-done(((bf16[56,832]{1,0:T(8,128)(2,1)}), bf16[896,832]{1,0:T(8,128)(2,1)}) %all-gather.2.cloned.1.call-update) | async-done | bytes 1490960 | tf_op jit(solution)/shard_map/all_gather | solution.py:27
  630.9 3.5 copy.8
Async XLA Ops:
  7.2 536.2 %all-reduce.2.cloned.1.call-start = ((), (), s32[]{:S(2)}) async-start(), calls=%async_computation | async-start | bytes 3407872 | tf_op jit(solution)/shard_map/psum | solution.py:20
  81.1 549.8 %all-gather.2.cloned.1.call-start = ((), (), s32[]{:S(2)}) async-start(), calls=%async_computation.1 | async-start | bytes 1705984 | tf_op jit(solution)/shard_map/all_gather | solution.py:27
  81.2 462.2 %copy-start = (bf16[56,512]{1,0:T(8,128)(2,1)S(1)}, bf16[56,512]{1,0:T(8,128)(2,1)}, u32[]{:S(2)}) copy-start(bf16[56,512]{1,0:T(8,128)(2,1)} %param.7) | copy-start | bytes 172036
  81.2 462.2 %copy-start.1 = (f32[56,832]{1,0:T(8,128)S(1)}, f32[56,832]{1,0:T(8,128)}, u32[]{:S(2)}) copy-start(f32[56,832]{1,0:T(8,128)} %param.6) | copy-start | bytes 559108
Sparse Core Ops, SparseCore 0:
  81.2 462.0 all-reduce.1
  547.3 83.6 all-gather.1
where the time goes:
time: 642 us; the launch traced here: 641 us
  waiting for transfers between devices  545 us (85%)
  blocking collectives  62.8 us (10%)
  between operations  14.1 us (2%)
  local copies, waits for them, and re-layouts  9.28 us (1%)
  matrix products  8.51 us (1%)
    psum x1, waiting for transfers between devices, shards(): sketch = lax.psum(partial_sketch, ('rep', 'fsdp')) / groups  460 us
    all_gather x1, waiting for transfers between devices, shards(): new_weights = lax.all_gather(updated, 'rep', axis=0, tiled=True)  84.4 us
    all_gather x1, blocking collectives, shards(): lax.all_gather(sketch_matrix, 'rep', axis=0, tiled=True).astype(jnp.float32)  62.8 us
  transfers between devices with their start and end apart: 2, of which 2 were waited for; matrix products, arithmetic and copies ran while one was open for 0% of the time, Pallas kernels for 0%

commit v1 on v0

v1 whole, which is shorter than its diff:
```python
import jax
import jax.numpy as jnp
import numpy as np
from jax import lax
from jax.sharding import Mesh, PartitionSpec as P

REP = ("zhi", "y", "core")
FSDP = ("zlo", "x")
PLANE = ("y", "core")
SUMMED = ("zhi", "zlo", "x")
ALL = REP + FSDP
SIZES = (2, 4, 2, 8, 4)
GROUPS = 16
CUTS = 8
HIGHEST = lax.Precision.HIGHEST


def swapped(axis):
    index = np.arange(int(np.prod(SIZES))).reshape(SIZES)
    other = np.flip(index, axis=ALL.index(axis))
    return [(int(a), int(b)) for a, b in zip(index.ravel(), other.ravel())]


def swap(value, axis):
    return lax.ppermute(value, ALL, swapped(axis))


def in_order(own, other, axis, at):
    first = lax.axis_index(axis) == 0
    return jnp.stack([jnp.where(first, own, other), jnp.where(first, other, own)], axis=at)


def spread(value, axes, parts):
    return lax.all_to_all(jnp.broadcast_to(value[None], (parts,) + value.shape), axes, 0, 0, tiled=True)


def shards(base_weights, local_weights, momentum, sketch_matrix):
    rows, width = momentum.shape
    rank = sketch_matrix.shape[1]
    cols = width // CUTS
    held = base_weights.shape[0]
    cut = lax.axis_index(PLANE)

    with jax.named_scope("sketch_rows_zhi"):
        sketch_pair = in_order(sketch_matrix, swap(sketch_matrix, "zhi"), "zhi", 0)
    with jax.named_scope("momentum_rows_zhi"):
        momentum_pair = in_order(momentum, swap(momentum, "zhi"), "zhi", 0)
    with jax.named_scope("local_columns"):
        local_cols = lax.all_to_all(local_weights[0].T.reshape(CUTS, cols, held), PLANE, 0, 0, tiled=True)
    with jax.named_scope("sketch_rows_plane"):
        gathered = lax.all_gather(sketch_pair.reshape(2 * rows, rank), PLANE, axis=0, tiled=False)
        gauss = gathered.reshape(CUTS, 2, rows, rank).transpose(1, 0, 2, 3).reshape(held, rank).astype(jnp.float32)
    with jax.named_scope("momentum_columns"):
        pieces = momentum_pair.reshape(2 * rows, CUTS, cols).transpose(1, 0, 2)
        pieces = lax.all_to_all(pieces, PLANE, 0, 0, tiled=True).reshape(CUTS, 2, rows, cols)
        momentum_cols = pieces.transpose(1, 0, 2, 3).reshape(held, cols).T
    with jax.named_scope("drift"):
        base_cols = lax.dynamic_slice_in_dim(base_weights.T, cut * cols, cols, 0).astype(jnp.float32)
        drift = jnp.sum(base_cols[None] - local_cols.astype(jnp.float32), axis=0)
    with jax.named_scope("partial_sketch"):
        partial = jnp.dot(drift, gauss, precision=HIGHEST, preferred_element_type=jnp.float32)
    with jax.named_scope("sketch_sum"):
        padded = jnp.pad(partial, ((0, 128 - cols), (0, 0)))
        tiles = padded.reshape(16, 8, 4, 128).transpose(0, 2, 1, 3).reshape(64, 8, 128)
        mine = jnp.sum(lax.all_to_all(tiles, SUMMED, 0, 0, tiled=True), axis=0)
        tiles = spread(mine, SUMMED, 64).reshape(16, 4, 8, 128)
        sketch = tiles.transpose(0, 2, 1, 3).reshape(128, rank)[:cols] / GROUPS
    with jax.named_scope("decode"):
        decoded = lax.dot_general(
            sketch, gauss, (((1,), (1,)), ((), ())), precision=HIGHEST, preferred_element_type=jnp.float32
        )
        stepped = 0.9 * momentum_cols + decoded
        updated = (base_cols - 0.7 * (decoded + 0.9 * stepped)).astype(jnp.bfloat16)
    with jax.named_scope("weights_y"):
        over_y = spread(updated, "y", 4)
    with jax.named_scope("weights_core"):
        both = in_order(over_y, swap(over_y, "core"), "core", 1)
        new_weights = both.reshape(width, held).T
    with jax.named_scope("decoded_rows"):
        plane_rows = lax.dynamic_slice_in_dim(decoded, lax.axis_index("zhi") * (held // 2), held // 2, 1)
        plane_rows = plane_rows.T.reshape(CUTS, rows, cols)
        back = lax.all_to_all(plane_rows, PLANE, 0, 0, tiled=True)
        new_momentum = 0.9 * momentum + back.transpose(1, 0, 2).reshape(rows, width)
    return new_weights, new_momentum


def solution(mesh):
    fine = Mesh(mesh.devices.reshape(SIZES), ALL)
    placed = (P(FSDP, None), P(REP, FSDP, None), P(FSDP + REP, None), P(FSDP + REP, None))
    return jax.shard_map(
        shards,
        mesh=fine,
        in_specs=placed,
        out_specs=(P(FSDP, None), P(FSDP + REP, None)),
        check_vma=False,
    )
```

time: 642 us -> 161 us (0.25)
  waiting for transfers between devices: 545 us -> 11.6 us
  starting transfers between devices: 0.08 us -> 43.2 us
  blocking collectives: 62.8 us -> 96.5 us
  between operations: 14.1 us -> 0.85 us
  local copies, waits for them, and re-layouts: 9.28 us -> 2.14 us
  matrix products: 8.51 us -> 1.52 us
    psum x1 -> x0, waiting for transfers between devices: 460 us -> none  [shards(): sketch = lax.psum(partial_sketch, ('rep', 'fsdp')) / groups]
    all_gather x1 -> x0, waiting for transfers between devices: 84.4 us -> none  [shards(): new_weights = lax.all_gather(updated, 'rep', axis=0, tiled=True)]
    all_to_all x0 -> x4, blocking collectives: none -> 81.2 us  [the longest x1 37.3 us: shards(): mine = jnp.sum(lax.all_to_all(tiles, SUMMED, 0, 0, tiled=True), axis=0)]
    all_gather x1, blocking collectives: 62.8 us -> 15.3 us  [shards(): lax.all_gather(sketch_pair.reshape(2 * rows, rank), PLANE, axis=0, tiled=...]
    ppermute x0 -> x3, starting transfers between devices: none -> 26.5 us  [swap(): return lax.ppermute(value, ALL, swapped(axis))]
    all_to_all x0 -> x2, starting transfers between devices: none -> 16.7 us  [the longest x1 10.5 us: shards(): lax.all_to_all(local_weights[0].T.reshape(CUTS, cols, held), PLANE, 0, 0,...]
    unnamed x7 -> x4, local copies, waits for them, and re-layouts: 9.28 us -> 0.01 us
    dot_general x2, matrix products: 8.51 us -> 1.52 us  [the longest x1 0.95 us: shards(): lax.dot_general(sketch, gauss, (((1,), (1,)), ((), ())), precision=HIGHES...]
  transfers between devices with their start and end apart: 2 -> 5, of which waited for: 2 -> 4; matrix products, arithmetic and copies ran while one was open for 0% -> 2% of each run, Pallas kernels for 0% -> 0%
where the time goes in v1:
time: 161 us; the launch traced here: 160 us
  blocking collectives  96.5 us (60%)
  starting transfers between devices  43.2 us (27%)
  waiting for transfers between devices  11.6 us (7%)
  other arithmetic  4.58 us (3%)
  local copies, waits for them, and re-layouts  2.14 us (1%)
    all_to_all x1, blocking collectives, shards(): mine = jnp.sum(lax.all_to_all(tiles, SUMMED, 0, 0, tiled=True), axis=0)  37.3 us
    ppermute x3, starting transfers between devices, swap(): return lax.ppermute(value, ALL, swapped(axis))  26.5 us
    all_to_all x1, blocking collectives, shards(): back = lax.all_to_all(plane_rows, PLANE, 0, 0, tiled=True)  17.6 us
    all_gather x1, blocking collectives, shards(): lax.all_gather(sketch_pair.reshape(2 * rows, rank), PLANE, axis=0, tiled=...  15.3 us
    all_to_all x1, blocking collectives, spread(): lax.all_to_all(jnp.broadcast_to(value[None], (parts,) + value.shape), axe...  13.4 us
    all_to_all x1, blocking collectives, shards(): lax.all_to_all(pieces, PLANE, 0, 0, tiled=True).reshape(CUTS, 2, rows, cols)  12.9 us
    all_to_all x1, starting transfers between devices, shards(): lax.all_to_all(local_weights[0].T.reshape(CUTS, cols, held), PLANE, 0, 0,...  10.5 us
    all_to_all x1, waiting for transfers between devices, spread(): lax.all_to_all(jnp.broadcast_to(value[None], (parts,) + value.shape), axe...  6.98 us
  transfers between devices with their start and end apart: 5, of which 4 were waited for; matrix products, arithmetic and copies ran while one was open for 2% of the time, Pallas kernels for 0%

profile of v1, /device:TPU:1, one launch (start us, length us, event | category | flops | bytes accessed | tf_op | source)
XLA Modules:
  0.0 160.4 jit_solution(12617374525966836961)
XLA Ops:
  0.6 10.5 %all-to-all-start = ((bf16[8,104,896]{2,1,0:T(8,128)(2,1)}), bf16[8,104,896]{2,1,0:T(8,128)(2,1)S(1)}, u32[]{:S(2)}, u32[]{:S(2)}) async-start(bf16[8,104,896]{2,1,0:T(8,128)(2,1)} %bitcast.72), calls=%async_computation | async-start | bytes 2981888 | tf_op jit(solution)/shard_map/local_columns/all_to_all | solution.py:49
  11.1 11.0 %collective-permute-start = (bf16[56,512]{1,0:T(8,128)(2,1)S(1)}, bf16[56,512]{1,0:T(8,128)(2,1)S(1)}, u32[]{:S(2)}, u32[]{:S(2)}) collective-permute-start(bf16[56,512]{1,0:T(8,128)(2,1)S(1)} %copy-done.1), channel_id=1, source_target_pairs={{0,256},{1,257},{2,258},{3,259},{4,260},{5,261},{6,262},{7,263},{8... | collective-permute-start | bytes 172040 | tf_op jit(solution)/shard_map/sketch_rows_zhi/ppermute | solution.py:25
  22.2 1.0 convert_bitcast_fusion
  23.2 2.0 %collective-permute-done = bf16[56,512]{1,0:T(8,128)(2,1)S(1)} collective-permute-done((bf16[56,512]{1,0:T(8,128)(2,1)S(1)}, bf16[56,512]{1,0:T(8,128)(2,1)S(1)}, u32[]{:S(2)}, u32[]{:S(2)}) %collective-permute-start) | collective-permute-done | bytes 57376 | tf_op jit(solution)/shard_map/sketch_rows_zhi/ppermute | solution.py:25
  25.2 15.3 %all_gather.3 = bf16[8,112,512]{2,1,0:T(8,128)(2,1)S(1)} all-gather(bf16[1,112,512]{2,1,0:T(8,128)(2,1)S(1)} %bitcast.78), channel_id=1, replica_groups=mesh['zhi'=2,'y'=4,'core'=2,'zlo'=8,'x'=4] {'y','core'}, dimensions={0}, use_global_device_ids=true | all-gather | bytes 1032192 | tf_op jit(solution)/shard_map/sketch_rows_plane/all_gather | solution.py:51
  40.5 0.3 subtract_reduce_fusion
  40.8 0.6 fusion.10
  41.4 37.3 %all_to_all.30 = f32[64,8,128]{2,1,0:T(8,128)S(1)} all-to-all(f32[64,8,128]{2,1,0:T(8,128)S(1)} %bitcast.74), channel_id=1, replica_groups=mesh['zhi'=2,'y'=4,'core'=2,'zlo'=8,'x'=4] {'zhi','zlo','x'}, dimensions={0} | all-to-all | bytes 524288 | tf_op jit(solution)/shard_map/sketch_sum/all_to_all | solution.py:65
  78.7 0.7 broadcast_in_dim.4
  79.5 6.2 %all-to-all-start.2 = ((f32[64,8,128]{2,1,0:T(8,128)}), f32[64,8,128]{2,1,0:T(8,128)S(1)}, u32[]{:S(2)}, u32[]{:S(2)}) async-start(f32[64,8,128]{2,1,0:T(8,128)} %broadcast_in_dim.4), calls=%async_computation.2 | async-start | bytes 524288 | tf_op jit(solution)/shard_map/sketch_sum/all_to_all | solution.py:34
  85.7 11.7 %collective-permute-start.1 = (f32[56,832]{1,0:T(8,128)S(1)}, f32[56,832]{1,0:T(8,128)S(1)}, u32[]{:S(2)}, u32[]{:S(2)}) collective-permute-start(f32[56,832]{1,0:T(8,128)S(1)} %copy-done), channel_id=1, source_target_pairs={{0,256},{1,257},{2,258},{3,259},{4,260},{5,261},{6,262},{7,263},{8... | collective-permute-start | bytes 559112 | tf_op jit(solution)/shard_map/momentum_rows_zhi/ppermute | solution.py:25
  97.5 7.0 %all-to-all-done.2 = f32[64,8,128]{2,1,0:T(8,128)S(1)} async-done(((f32[64,8,128]{2,1,0:T(8,128)}), f32[64,8,128]{2,1,0:T(8,128)S(1)}, u32[]{:S(2)}, u32[]{:S(2)}) %all-to-all-start.2) | async-done | bytes 262176 | tf_op jit(solution)/shard_map/sketch_sum/all_to_all | solution.py:34
  104.4 1.0 fusion.6
  105.7 17.6 %all_to_all.31 = f32[8,56,104]{2,1,0:T(8,128)S(1)} all-to-all(f32[8,56,104]{2,1,0:T(8,128)S(1)} %bitcast.75), channel_id=1, replica_groups=mesh['zhi'=2,'y'=4,'core'=2,'zlo'=8,'x'=4] {'y','core'}, dimensions={0} | all-to-all | bytes 372736 | tf_op jit(solution)/shard_map/decoded_rows/all_to_all | solution.py:82
  123.5 0.9 collective-permute-done.1
  124.3 0.7 select_bitcast_fusion.3
  125.1 0.2 reshape.56
  125.3 0.2 copy.21
  125.5 12.9 %all_to_all.32 = f32[8,112,104]{1,2,0:T(8,128)S(1)} all-to-all(f32[8,112,104]{1,2,0:T(8,128)S(1)} %copy.21), channel_id=1, replica_groups=mesh['zhi'=2,'y'=4,'core'=2,'zlo'=8,'x'=4] {'y','core'}, dimensions={0} | all-to-all | bytes 745472 | tf_op jit(solution)/shard_map/momentum_columns/all_to_all | solution.py:55
  139.0 1.0 fusion.4
  140.1 13.4 %all_to_all.33 = bf16[4,104,896]{2,1,0:T(8,128)(2,1)S(1)} all-to-all(bf16[4,104,896]{2,1,0:T(8,128)(2,1)S(1)} %broadcast_in_dim.5), channel_id=1, replica_groups=mesh['zhi'=2,'y'=4,'core'=2,'zlo'=8,'x'=4] {'y'}, dimensions={0} | all-to-all | bytes 1490944 | tf_op jit(solution)/shard_map/weights_y/all_to_all | solution.py:34
  153.4 3.7 %collective-permute-start.2 = (bf16[4,104,896]{2,1,0:T(8,128)(2,1)S(1)}, bf16[4,104,896]{2,1,0:T(8,128)(2,1)S(1)}, u32[]{:S(2)}, u32[]{:S(2)}) collective-permute-start(bf16[4,104,896]{2,1,0:T(8,128)(2,1)S(1)} %all_to_all.33), channel_id=1, source_target_pairs={{0,32},{1,33},{2,34},{3,35},{4,36},{5,37},{6,38},{7,39},{8,40},{9,... | collective-permute-start | bytes 2236424 | tf_op jit(solution)/shard_map/weights_core/ppermute | solution.py:25
  157.2 1.8 %collective-permute-done.2 = bf16[4,104,896]{2,1,0:T(8,128)(2,1)S(1)} collective-permute-done((bf16[4,104,896]{2,1,0:T(8,128)(2,1)S(1)}, bf16[4,104,896]{2,1,0:T(8,128)(2,1)S(1)}, u32[]{:S(2)}, u32[]{:S(2)}) %collective-permute-start.2) | collective-permute-done | bytes 745504 | tf_op jit(solution)/shard_map/weights_core/ppermute | solution.py:25
  159.1 1.3 pad_maximum_fusion
  (21 shorter events, 1.3 us)
Async XLA Ops:
  0.6 10.5 %copy-start.1 = (bf16[56,512]{1,0:T(8,128)(2,1)S(1)}, bf16[56,512]{1,0:T(8,128)(2,1)}, u32[]{:S(2)}) copy-start(bf16[56,512]{1,0:T(8,128)(2,1)} %param.7) | copy-start | bytes 172036
  0.6 39.9 %all-to-all-start = ((bf16[8,104,896]{2,1,0:T(8,128)(2,1)}), bf16[8,104,896]{2,1,0:T(8,128)(2,1)S(1)}, u32[]{:S(2)}, u32[]{:S(2)}) async-start(bf16[8,104,896]{2,1,0:T(8,128)(2,1)} %bitcast.72), calls=%async_computation | async-start | bytes 2981888 | tf_op jit(solution)/shard_map/local_columns/all_to_all | solution.py:49
  11.1 14.0 %collective-permute-start = (bf16[56,512]{1,0:T(8,128)(2,1)S(1)}, bf16[56,512]{1,0:T(8,128)(2,1)S(1)}, u32[]{:S(2)}, u32[]{:S(2)}) collective-permute-start(bf16[56,512]{1,0:T(8,128)(2,1)S(1)} %copy-done.1), channel_id=1, source_target_pairs={{0,256},{1,257},{2,258},{3,259},{4,260},{5,261},{6,262},{7,263},{8... | collective-permute-start | bytes 172040 | tf_op jit(solution)/shard_map/sketch_rows_zhi/ppermute | solution.py:25
  40.8 44.9 %copy-start = (f32[56,832]{1,0:T(8,128)S(1)}, f32[56,832]{1,0:T(8,128)}, u32[]{:S(2)}) copy-start(f32[56,832]{1,0:T(8,128)} %param.6) | copy-start | bytes 559108
  79.5 25.0 %all-to-all-start.2 = ((f32[64,8,128]{2,1,0:T(8,128)}), f32[64,8,128]{2,1,0:T(8,128)S(1)}, u32[]{:S(2)}, u32[]{:S(2)}) async-start(f32[64,8,128]{2,1,0:T(8,128)} %broadcast_in_dim.4), calls=%async_computation.2 | async-start | bytes 524288 | tf_op jit(solution)/shard_map/sketch_sum/all_to_all | solution.py:34
  85.7 38.6 %collective-permute-start.1 = (f32[56,832]{1,0:T(8,128)S(1)}, f32[56,832]{1,0:T(8,128)S(1)}, u32[]{:S(2)}, u32[]{:S(2)}) collective-permute-start(f32[56,832]{1,0:T(8,128)S(1)} %copy-done), channel_id=1, source_target_pairs={{0,256},{1,257},{2,258},{3,259},{4,260},{5,261},{6,262},{7,263},{8... | collective-permute-start | bytes 559112 | tf_op jit(solution)/shard_map/momentum_rows_zhi/ppermute | solution.py:25
  153.4 5.6 %collective-permute-start.2 = (bf16[4,104,896]{2,1,0:T(8,128)(2,1)S(1)}, bf16[4,104,896]{2,1,0:T(8,128)(2,1)S(1)}, u32[]{:S(2)}, u32[]{:S(2)}) collective-permute-start(bf16[4,104,896]{2,1,0:T(8,128)(2,1)S(1)} %all_to_all.33), channel_id=1, source_target_pairs={{0,32},{1,33},{2,34},{3,35},{4,36},{5,37},{6,38},{7,39},{8,40},{9,... | collective-permute-start | bytes 2236424 | tf_op jit(solution)/shard_map/weights_core/ppermute | solution.py:25

commit v2 on v1

v2 whole, which is shorter than its diff:
```python
import jax
import jax.numpy as jnp
import numpy as np
from jax import lax
from jax.sharding import Mesh, PartitionSpec as P

REP = ("zhi", "y", "core")
FSDP = ("zm", "zn", "x")
PLANE = ("y", "core")
NEAR = ("zn", "x")
FAR = ("zhi", "zm")
ALL = REP + FSDP
SIZES = (2, 4, 2, 2, 4, 4)
GROUPS = 16
CUTS = 8
HIGHEST = lax.Precision.HIGHEST


def swapped(axis):
    index = np.arange(int(np.prod(SIZES))).reshape(SIZES)
    other = np.flip(index, axis=ALL.index(axis))
    return [(int(a), int(b)) for a, b in zip(index.ravel(), other.ravel())]


def swap(value, axis):
    return lax.ppermute(value, ALL, swapped(axis))


def in_order(own, other, axis, at):
    first = lax.axis_index(axis) == 0
    return jnp.stack([jnp.where(first, own, other), jnp.where(first, other, own)], axis=at)


def spread(value, axes, parts):
    return lax.all_to_all(jnp.broadcast_to(value[None], (parts,) + value.shape), axes, 0, 0, tiled=True)


def halves(value):
    high = lax.reduce_precision(value, 8, 7)
    return high.astype(jnp.bfloat16), (value - high).astype(jnp.bfloat16)


def joined(high, low):
    return high.astype(jnp.float32) + low.astype(jnp.float32)


def wide(value, lanes):
    return jnp.pad(value, [(0, 0)] * (value.ndim - 1) + [(0, lanes - value.shape[-1])])


def shards(base_weights, local_weights, momentum, sketch_matrix):
    rows, width = momentum.shape
    rank = sketch_matrix.shape[1]
    cols = width // CUTS
    held = base_weights.shape[0]
    cut = lax.axis_index(PLANE)

    with jax.named_scope("sketch_rows_zhi"):
        sketch_pair = in_order(sketch_matrix, swap(sketch_matrix, "zhi"), "zhi", 0)
    with jax.named_scope("local_and_momentum_columns"):
        high, low = halves(momentum.T)
        sent = jnp.concatenate([local_weights[0].T, high, low], axis=1)
        got = lax.all_to_all(wide(sent, 1024).reshape(CUTS, cols, 1024), PLANE, 0, 0, tiled=True)
    with jax.named_scope("sketch_rows_plane"):
        gathered = lax.all_gather(sketch_pair.reshape(2 * rows, rank), PLANE, axis=0, tiled=False)
        gauss = gathered.reshape(CUTS, 2, rows, rank).transpose(1, 0, 2, 3).reshape(held, rank).astype(jnp.float32)
    with jax.named_scope("drift"):
        base_cols = lax.dynamic_slice_in_dim(base_weights.T, cut * cols, cols, 0).astype(jnp.float32)
        drift = jnp.sum(base_cols[None] - got[:, :, :held].astype(jnp.float32), axis=0)
    with jax.named_scope("partial_sketch"):
        partial = jnp.dot(drift, gauss, precision=HIGHEST, preferred_element_type=jnp.float32)
    with jax.named_scope("momentum_columns_zhi"):
        own = joined(got[:, :, held : held + rows], got[:, :, held + rows : held + 2 * rows])
        own = own.transpose(1, 0, 2).reshape(cols, held // 2)
        other = swap((own * 8192.0).astype(jnp.float16), "zhi").astype(jnp.float32) / 8192.0
        momentum_cols = in_order(own, other, "zhi", 1).reshape(cols, held)
    with jax.named_scope("sketch_sum"):
        padded = jnp.pad(partial, ((0, 128 - cols), (0, 0)))
        mine = jnp.sum(lax.all_to_all(padded.reshape(16, 8, rank), NEAR, 0, 0, tiled=True), axis=0)
        mine = jnp.sum(spread(mine, FAR, 4), axis=0)
        mine, momentum_cols = lax.optimization_barrier((mine, momentum_cols))
        sketch = spread(mine, NEAR, 16).reshape(128, rank)[:cols] / GROUPS
    with jax.named_scope("decode"):
        decoded = lax.dot_general(
            sketch, gauss, (((1,), (1,)), ((), ())), precision=HIGHEST, preferred_element_type=jnp.float32
        )
        stepped = 0.9 * momentum_cols + decoded
        updated = (base_cols - 0.7 * (decoded + 0.9 * stepped)).astype(jnp.bfloat16)
    with jax.named_scope("weights_y"):
        plane_rows = lax.dynamic_slice_in_dim(decoded, lax.axis_index("zhi") * (held // 2), held // 2, 1)
        high, low = halves(plane_rows.reshape(cols, 4, 2, rows).transpose(1, 2, 0, 3))
        pieces = jnp.concatenate([high, low], axis=3)
        copies = jnp.broadcast_to(updated[None], (4, cols, held))
        sent = jnp.concatenate([copies, wide(pieces[:, 0], 128), wide(pieces[:, 1], 128)], axis=2)
        over_y = lax.all_to_all(sent, "y", 0, 0, tiled=True)
    with jax.named_scope("weights_core"):
        first = lax.axis_index("core") == 0
        kept, given = over_y[:, :, held : held + 128], over_y[:, :, held + 128 :]
        kept, given = jnp.where(first, kept, given), jnp.where(first, given, kept)
        own = jnp.concatenate([over_y[:, :, :held], kept], axis=2)
        other = swap(jnp.concatenate([over_y[:, :, :held], given], axis=2), "core")
        both = in_order(own, other, "core", 1)
        new_weights = both[..., :held].reshape(width, held).T
    with jax.named_scope("new_momentum"):
        back = joined(both[..., held : held + rows], both[..., held + rows : held + 2 * rows])
        new_momentum = 0.9 * momentum + back.reshape(width, rows).T
    return new_weights, new_momentum


def solution(mesh):
    fine = Mesh(mesh.devices.reshape(SIZES), ALL)
    placed = (P(FSDP, None), P(REP, FSDP, None), P(FSDP + REP, None), P(FSDP + REP, None))
    return jax.shard_map(
        shards,
        mesh=fine,
        in_specs=placed,
        out_specs=(P(FSDP, None), P(FSDP + REP, None)),
        check_vma=False,
    )
```

time: 161 us -> 141 us (0.88)
  blocking collectives: 96.5 us -> 17.6 us
  starting transfers between devices: 43.2 us -> 72.4 us
  waiting for transfers between devices: 11.6 us -> 33.6 us
  other arithmetic: 4.58 us -> 8.03 us
  local copies, waits for them, and re-layouts: 2.14 us -> 5.43 us
    all_to_all x4 -> x0, blocking collectives: 81.2 us -> none  [the longest x1 37.3 us: shards(): mine = jnp.sum(lax.all_to_all(tiles, SUMMED, 0, 0, tiled=True), axis=0)]
    all_to_all x1 -> x2, waiting for transfers between devices: 6.98 us -> 20.4 us  [spread(): lax.all_to_all(jnp.broadcast_to(value[None], (parts,) + value.shape), axe...]
    all_to_all x1 -> x3, starting transfers between devices: 10.5 us -> 22.3 us  [the longest x1 10.5 us: shards(): lax.all_to_all(wide(sent, 1024).reshape(CUTS, cols, 1024), PLANE, 0, 0, t...]
    all_to_all x1 -> x2, starting transfers between devices: 6.24 us -> 15.8 us  [spread(): lax.all_to_all(jnp.broadcast_to(value[None], (parts,) + value.shape), axe...]
    all_to_all x1 -> x3, waiting for transfers between devices: 0.01 us -> 9.27 us  [the longest x1 9.26 us: shards(): over_y = lax.all_to_all(sent, 'y', 0, 0, tiled=True)]
    ppermute x3, starting transfers between devices: 26.5 us -> 34.3 us  [swap(): return lax.ppermute(value, ALL, swapped(axis))]
    concatenate x0 -> x3, other arithmetic: none -> 4.02 us  [the longest x1 2.88 us: shards(): sent = jnp.concatenate([local_weights[0].T, high, low], axis=1)]
    all_gather x1, blocking collectives: 15.3 us -> 17.6 us  [shards(): lax.all_gather(sketch_pair.reshape(2 * rows, rank), PLANE, axis=0, tiled=...]
  transfers between devices with their start and end apart: 5 -> 8, of which waited for: 4 -> 5; matrix products, arithmetic and copies ran while one was open for 2% -> 2% of each run, Pallas kernels for 0% -> 0%
where the time goes in v2:
time: 141 us; the launch traced here: 140 us
  starting transfers between devices  72.4 us (51%)
  waiting for transfers between devices  33.6 us (24%)
  blocking collectives  17.6 us (12%)
  other arithmetic  8.03 us (6%)
  local copies, waits for them, and re-layouts  5.43 us (4%)
  matrix products  2.47 us (2%)
    ppermute x3, starting transfers between devices, swap(): return lax.ppermute(value, ALL, swapped(axis))  34.3 us
    all_to_all x2, waiting for transfers between devices, spread(): lax.all_to_all(jnp.broadcast_to(value[None], (parts,) + value.shape), axe...  20.4 us
    all_gather x1, blocking collectives, shards(): lax.all_gather(sketch_pair.reshape(2 * rows, rank), PLANE, axis=0, tiled=...  17.6 us
    all_to_all x2, starting transfers between devices, spread(): lax.all_to_all(jnp.broadcast_to(value[None], (parts,) + value.shape), axe...  15.8 us
    all_to_all x1, starting transfers between devices, shards(): lax.all_to_all(wide(sent, 1024).reshape(CUTS, cols, 1024), PLANE, 0, 0, t...  10.5 us
    all_to_all x1, waiting for transfers between devices, shards(): over_y = lax.all_to_all(sent, 'y', 0, 0, tiled=True)  9.26 us
    all_to_all x1, starting transfers between devices, shards(): over_y = lax.all_to_all(sent, 'y', 0, 0, tiled=True)  8.04 us
    ppermute x3, waiting for transfers between devices, swap(): return lax.ppermute(value, ALL, swapped(axis))  3.95 us
  transfers between devices with their start and end apart: 8, of which 5 were waited for; matrix products, arithmetic and copies ran while one was open for 2% of the time, Pallas kernels for 0%

profile of v2, /device:TPU:1, one launch (start us, length us, event | category | flops | bytes accessed | tf_op | source)
XLA Modules:
  0.0 140.4 jit_solution(6967315204953303227)
XLA Ops:
  0.6 1.0 reduce-precision_convert_fusion.1
  1.9 2.9 %fusion.7 = bf16[832,1024]{1,0:T(8,128)(2,1)} fusion(bf16[832,56]{1,0:T(8,128)(2,1)S(1)} %copy.44, bf16[832,56]{1,0:T(8,128)(2,1)S(1)} %copy.43, bf16[832,896]{1,0:T(8,128)(2,1)} %bitcast.64), kind=kLoop, calls=%fused_computation.16 | loop fusion | flops 8519680 | bytes 3381248 | tf_op jit(solution)/shard_map/local_and_momentum_columns/concatenate | solution.py:62
  4.8 10.5 %all-to-all-start = ((bf16[8,104,1024]{2,1,0:T(8,128)(2,1)}), bf16[8,104,1024]{2,1,0:T(8,128)(2,1)S(1)}, u32[]{:S(2)}, u32[]{:S(2)}) async-start(bf16[8,104,1024]{2,1,0:T(8,128)(2,1)} %bitcast.61), calls=%async_computation | async-start | bytes 3407872 | tf_op jit(solution)/shard_map/local_and_momentum_columns/all_to_all | solution.py:63
  15.3 11.0 %collective-permute-start = (bf16[56,512]{1,0:T(8,128)(2,1)S(1)}, bf16[56,512]{1,0:T(8,128)(2,1)S(1)}, u32[]{:S(2)}, u32[]{:S(2)}) collective-permute-start(bf16[56,512]{1,0:T(8,128)(2,1)S(1)} %copy-done.1), channel_id=1, source_target_pairs={{0,256},{1,257},{2,258},{3,259},{4,260},{5,261},{6,262},{7,263},{8... | collective-permute-start | bytes 172040 | tf_op jit(solution)/shard_map/sketch_rows_zhi/ppermute | solution.py:26
  26.4 1.0 convert_bitcast_fusion
  27.3 2.0 %collective-permute-done = bf16[56,512]{1,0:T(8,128)(2,1)S(1)} collective-permute-done((bf16[56,512]{1,0:T(8,128)(2,1)S(1)}, bf16[56,512]{1,0:T(8,128)(2,1)S(1)}, u32[]{:S(2)}, u32[]{:S(2)}) %collective-permute-start) | collective-permute-done | bytes 57376 | tf_op jit(solution)/shard_map/sketch_rows_zhi/ppermute | solution.py:26
  29.3 17.6 %all_gather.3 = bf16[8,112,512]{2,1,0:T(8,128)(2,1)S(1)} all-gather(bf16[1,112,512]{2,1,0:T(8,128)(2,1)S(1)} %bitcast.69), channel_id=1, replica_groups=mesh['zhi'=2,'y'=4,'core'=2,'zm'=2,'zn'=4,'x'=4] {'y','core'}, dimensions={0}, use_global_device_ids=true | all-gather | bytes 1032192 | tf_op jit(solution)/shard_map/sketch_rows_plane/all_gather | solution.py:65
  47.9 0.7 pad_bitcast_fusion
  48.7 3.7 %all-to-all-start.1 = ((f32[16,8,512]{2,1,0:T(8,128)}), f32[16,8,512]{2,1,0:T(8,128)S(1)}, u32[]{:S(2)}, u32[]{:S(2)}) async-start(f32[16,8,512]{2,1,0:T(8,128)} %pad_bitcast_fusion), calls=%async_computation.1 | async-start | bytes 524288 | tf_op jit(solution)/shard_map/sketch_sum/all_to_all | solution.py:79
  52.7 13.0 %collective-permute-start.1 = (f16[104,448]{0,1:T(8,128)(2,1)S(1)}, f16[104,448]{0,1:T(8,128)(2,1)S(1)}, u32[]{:S(2)}, u32[]{:S(2)}) collective-permute-start(f16[104,448]{0,1:T(8,128)(2,1)S(1)} %fusion.12), channel_id=1, source_target_pairs={{0,256},{1,257},{2,258},{3,259},{4,260},{5,261},{6,262},{7,263},{8... | collective-permute-start | bytes 279560 | tf_op jit(solution)/shard_map/momentum_columns_zhi/ppermute | solution.py:26
  65.8 0.6 broadcast_in_dim.6
  66.4 9.1 %all-to-all-start.2 = ((f32[4,8,512]{2,1,0:T(8,128)}), f32[4,8,512]{2,1,0:T(8,128)S(1)}, u32[]{:S(2)}, u32[]{:S(2)}) async-start(f32[4,8,512]{2,1,0:T(8,128)} %broadcast_in_dim.6), calls=%async_computation.2 | async-start | bytes 131072 | tf_op jit(solution)/shard_map/sketch_sum/all_to_all | solution.py:35
  75.8 11.5 %all-to-all-done.2 = f32[4,8,512]{2,1,0:T(8,128)S(1)} async-done(((f32[4,8,512]{2,1,0:T(8,128)}), f32[4,8,512]{2,1,0:T(8,128)S(1)}, u32[]{:S(2)}, u32[]{:S(2)}) %all-to-all-start.2) | async-done | bytes 65568 | tf_op jit(solution)/shard_map/sketch_sum/all_to_all | solution.py:35
  87.3 0.7 broadcast_in_dim.7
  88.0 6.7 %all-to-all-start.3 = ((f32[16,8,512]{2,1,0:T(8,128)}), f32[16,8,512]{2,1,0:T(8,128)S(1)}, u32[]{:S(2)}, u32[]{:S(2)}) async-start(f32[16,8,512]{2,1,0:T(8,128)} %broadcast_in_dim.7), calls=%async_computation.3 | async-start | bytes 524288 | tf_op jit(solution)/shard_map/sketch_sum/all_to_all | solution.py:35
  94.8 8.9 %all-to-all-done.3 = f32[16,8,512]{2,1,0:T(8,128)S(1)} async-done(((f32[16,8,512]{2,1,0:T(8,128)}), f32[16,8,512]{2,1,0:T(8,128)S(1)}, u32[]{:S(2)}, u32[]{:S(2)}) %all-to-all-start.3) | async-done | bytes 262176 | tf_op jit(solution)/shard_map/sketch_sum/all_to_all | solution.py:35
  103.6 1.9 %subtract_convert_fusion = (bf16[104,896]{1,0:T(8,128)(2,1)S(1)}, f32[104,896]{1,0:T(8,128)S(1)}) fusion(f32[104,896]{1,0:T(8,128)S(1)} %copy.54, bf16[896,832]{0,1:T(8,128)(2,1)} %param.4, s32[]{:T(128)S(6)} %select_n.55, bf16[896,512]{1,0:T(8,128)(2,1)S(1)} %bitcast.60, f32[16,8,512]{2,1,0:T(8,128)S(1)} %all-to-all-done.3), kind=kOutput, calls=%fused_computation.28 | convolution fusion | flops 573321216 | bytes 2248708 | tf_op jit(solution)/shard_map/decode/dot_general | solution.py:84
  106.2 1.0 fusion.10
  107.2 8.0 %all-to-all-start.4 = ((bf16[4,104,1152]{2,1,0:T(8,128)(2,1)}), bf16[4,104,1152]{2,1,0:T(8,128)(2,1)S(1)}, u32[]{:S(2)}, u32[]{:S(2)}) async-start(bf16[4,104,1152]{2,1,0:T(8,128)(2,1)} %fusion.10), calls=%async_computation.4 | async-start | bytes 1916928 | tf_op jit(solution)/shard_map/weights_y/all_to_all | solution.py:95
  115.3 9.3 %all-to-all-done.4 = bf16[4,104,1152]{2,1,0:T(8,128)(2,1)S(1)} async-done(((bf16[4,104,1152]{2,1,0:T(8,128)(2,1)}), bf16[4,104,1152]{2,1,0:T(8,128)(2,1)S(1)}, u32[]{:S(2)}, u32[]{:S(2)}) %all-to-all-start.4) | async-done | bytes 958496 | tf_op jit(solution)/shard_map/weights_y/all_to_all | solution.py:95
  124.7 10.3 %collective-permute-start.2 = (bf16[4,104,1024]{2,1,0:T(8,128)(2,1)S(1)}, bf16[4,104,1024]{2,1,0:T(8,128)(2,1)S(1)}, u32[]{:S(2)}, u32[]{:S(2)}) collective-permute-start(bf16[4,104,1024]{2,1,0:T(8,128)(2,1)S(1)} %pad_maximum_fusion.1), channel_id=1, source_target_pairs={{0,32},{1,33},{2,34},{3,35},{4,36},{5,37},{6,38},{7,39},{8,40},{9,... | collective-permute-start | bytes 2555912 | tf_op jit(solution)/shard_map/weights_core/ppermute | solution.py:26
  135.0 2.0 %collective-permute-done.2 = bf16[4,104,1024]{2,1,0:T(8,128)(2,1)S(1)} collective-permute-done((bf16[4,104,1024]{2,1,0:T(8,128)(2,1)S(1)}, bf16[4,104,1024]{2,1,0:T(8,128)(2,1)S(1)}, u32[]{:S(2)}, u32[]{:S(2)}) %collective-permute-start.2) | collective-permute-done | bytes 852000 | tf_op jit(solution)/shard_map/weights_core/ppermute | solution.py:26
  138.5 0.7 bitcast_add_fusion
  139.2 1.2 copy.52
  (37 shorter events, 4.2 us)
Async XLA Ops:
  4.8 10.5 %copy-start.1 = (bf16[56,512]{1,0:T(8,128)(2,1)S(1)}, bf16[56,512]{1,0:T(8,128)(2,1)}, u32[]{:S(2)}) copy-start(bf16[56,512]{1,0:T(8,128)(2,1)} %param.7) | copy-start | bytes 172036
  4.8 42.2 %all-to-all-start = ((bf16[8,104,1024]{2,1,0:T(8,128)(2,1)}), bf16[8,104,1024]{2,1,0:T(8,128)(2,1)S(1)}, u32[]{:S(2)}, u32[]{:S(2)}) async-start(bf16[8,104,1024]{2,1,0:T(8,128)(2,1)} %bitcast.61), calls=%async_computation | async-start | bytes 3407872 | tf_op jit(solution)/shard_map/local_and_momentum_columns/all_to_all | solution.py:63
  15.3 14.0 %collective-permute-start = (bf16[56,512]{1,0:T(8,128)(2,1)S(1)}, bf16[56,512]{1,0:T(8,128)(2,1)S(1)}, u32[]{:S(2)}, u32[]{:S(2)}) collective-permute-start(bf16[56,512]{1,0:T(8,128)(2,1)S(1)} %copy-done.1), channel_id=1, source_target_pairs={{0,256},{1,257},{2,258},{3,259},{4,260},{5,261},{6,262},{7,263},{8... | collective-permute-start | bytes 172040 | tf_op jit(solution)/shard_map/sketch_rows_zhi/ppermute | solution.py:26
  48.7 17.1 %all-to-all-start.1 = ((f32[16,8,512]{2,1,0:T(8,128)}), f32[16,8,512]{2,1,0:T(8,128)S(1)}, u32[]{:S(2)}, u32[]{:S(2)}) async-start(f32[16,8,512]{2,1,0:T(8,128)} %pad_bitcast_fusion), calls=%async_computation.1 | async-start | bytes 524288 | tf_op jit(solution)/shard_map/sketch_sum/all_to_all | solution.py:79
  52.7 22.8 %collective-permute-start.1 = (f16[104,448]{0,1:T(8,128)(2,1)S(1)}, f16[104,448]{0,1:T(8,128)(2,1)S(1)}, u32[]{:S(2)}, u32[]{:S(2)}) collective-permute-start(f16[104,448]{0,1:T(8,128)(2,1)S(1)} %fusion.12), channel_id=1, source_target_pairs={{0,256},{1,257},{2,258},{3,259},{4,260},{5,261},{6,262},{7,263},{8... | collective-permute-start | bytes 279560 | tf_op jit(solution)/shard_map/momentum_columns_zhi/ppermute | solution.py:26
  66.4 20.9 %all-to-all-start.2 = ((f32[4,8,512]{2,1,0:T(8,128)}), f32[4,8,512]{2,1,0:T(8,128)S(1)}, u32[]{:S(2)}, u32[]{:S(2)}) async-start(f32[4,8,512]{2,1,0:T(8,128)} %broadcast_in_dim.6), calls=%async_computation.2 | async-start | bytes 131072 | tf_op jit(solution)/shard_map/sketch_sum/all_to_all | solution.py:35
  88.0 15.6 %all-to-all-start.3 = ((f32[16,8,512]{2,1,0:T(8,128)}), f32[16,8,512]{2,1,0:T(8,128)S(1)}, u32[]{:S(2)}, u32[]{:S(2)}) async-start(f32[16,8,512]{2,1,0:T(8,128)} %broadcast_in_dim.7), calls=%async_computation.3 | async-start | bytes 524288 | tf_op jit(solution)/shard_map/sketch_sum/all_to_all | solution.py:35
  107.2 17.3 %all-to-all-start.4 = ((bf16[4,104,1152]{2,1,0:T(8,128)(2,1)}), bf16[4,104,1152]{2,1,0:T(8,128)(2,1)S(1)}, u32[]{:S(2)}, u32[]{:S(2)}) async-start(bf16[4,104,1152]{2,1,0:T(8,128)(2,1)} %fusion.10), calls=%async_computation.4 | async-start | bytes 1916928 | tf_op jit(solution)/shard_map/weights_y/all_to_all | solution.py:95
  124.7 12.2 %collective-permute-start.2 = (bf16[4,104,1024]{2,1,0:T(8,128)(2,1)S(1)}, bf16[4,104,1024]{2,1,0:T(8,128)(2,1)S(1)}, u32[]{:S(2)}, u32[]{:S(2)}) collective-permute-start(bf16[4,104,1024]{2,1,0:T(8,128)(2,1)S(1)} %pad_maximum_fusion.1), channel_id=1, source_target_pairs={{0,32},{1,33},{2,34},{3,35},{4,36},{5,37},{6,38},{7,39},{8,40},{9,... | collective-permute-start | bytes 2555912 | tf_op jit(solution)/shard_map/weights_core/ppermute | solution.py:26
  137.5 0.9 copy-start

commit v3 on v2

v3 whole, which is shorter than its diff:
```python
import jax
import jax.numpy as jnp
import numpy as np
from jax import lax
from jax.sharding import Mesh, PartitionSpec as P

REP = ("zhi", "y", "core")
FSDP = ("zm", "zn", "x")
PLANE = ("y", "core")
NEAR = ("zn", "x")
FAR = ("zhi", "zm")
CUT = ("core", "y")
ALL = REP + FSDP
SIZES = (2, 4, 2, 2, 4, 4)
GROUPS = 16
CUTS = 8
CONTRACT = (((1,), (1,)), ((), ()))
HIGHEST = lax.Precision.HIGHEST


def swapped(axis):
    index = np.arange(int(np.prod(SIZES))).reshape(SIZES)
    other = np.flip(index, axis=ALL.index(axis))
    return [(int(a), int(b)) for a, b in zip(index.ravel(), other.ravel())]


def swap(value, axis):
    return lax.ppermute(value, ALL, swapped(axis))


def around_y(value):
    index = np.arange(int(np.prod(SIZES))).reshape(SIZES)
    got = [value]
    for step in (1, 2, 3):
        moved = np.roll(index, -step, axis=ALL.index("y"))
        got.append(lax.ppermute(value, ALL, [(int(a), int(b)) for a, b in zip(index.ravel(), moved.ravel())]))
    return jnp.roll(jnp.stack(got[::-1]), lax.axis_index("y") + 1, axis=0)


def in_order(own, other, axis, at):
    first = lax.axis_index(axis) == 0
    return jnp.stack([jnp.where(first, own, other), jnp.where(first, other, own)], axis=at)


def spread(value, axes, parts):
    return lax.all_to_all(jnp.broadcast_to(value[None], (parts,) + value.shape), axes, 0, 0, tiled=True)


def halves(value):
    high = lax.reduce_precision(value, 8, 7)
    return high.astype(jnp.bfloat16), (value - high).astype(jnp.bfloat16)


def joined(high, low):
    return high.astype(jnp.float32) + low.astype(jnp.float32)


def wide(value, lanes):
    return jnp.pad(value, [(0, 0)] * (value.ndim - 1) + [(0, lanes - value.shape[-1])])


def shards(base_weights, local_weights, momentum, sketch_matrix):
    rows, width = momentum.shape
    rank = sketch_matrix.shape[1]
    cols = width // CUTS
    held = base_weights.shape[0]
    cut = lax.axis_index(CUT)

    with jax.named_scope("sketch_rows_zhi"):
        sketch_pair = in_order(sketch_matrix, swap(sketch_matrix, "zhi"), "zhi", 0)
    with jax.named_scope("local_columns"):
        got = lax.all_to_all(local_weights[0].T.reshape(CUTS, cols, held), CUT, 0, 0, tiled=True)
    with jax.named_scope("sketch_rows_plane"):
        gathered = lax.all_gather(sketch_pair.reshape(2 * rows, rank), PLANE, axis=0, tiled=False)
        gauss = gathered.reshape(CUTS, 2, rows, rank).transpose(1, 0, 2, 3).reshape(held, rank)
    with jax.named_scope("drift"):
        base_cols = lax.dynamic_slice_in_dim(base_weights.T, cut * cols, cols, 0).astype(jnp.float32)
        drift = jnp.sum(base_cols[None] - got.astype(jnp.float32), axis=0)
    with jax.named_scope("partial_sketch"):
        partial = jnp.dot(drift, gauss.astype(jnp.float32), precision=HIGHEST, preferred_element_type=jnp.float32)
    with jax.named_scope("sketch_sum"):
        padded = jnp.pad(partial, ((0, 128 - cols), (0, 0)))
        mine = jnp.sum(lax.all_to_all(padded.reshape(16, 8, rank), NEAR, 0, 0, tiled=True), axis=0)
        mine, late = lax.optimization_barrier((mine, momentum))
        small = (late * 8192.0).astype(jnp.float16)
        momentum_pair = in_order(small, swap(small, "zhi"), "zhi", 0)
        momentum_y = around_y(momentum_pair.reshape(2 * rows, width))
        mine = jnp.sum(spread(mine, FAR, 4), axis=0)
        sketch = spread(mine, NEAR, 16).reshape(128, rank)[:cols] / GROUPS
    sketch, momentum_y = lax.optimization_barrier((sketch, momentum_y))
    with jax.named_scope("momentum_core"):
        momentum_all = in_order(momentum_y, swap(momentum_y, "core"), "core", 1)
    with jax.named_scope("prior"):
        known = momentum_all.reshape(CUTS, 2, rows, width).transpose(1, 0, 2, 3).reshape(held, width)
        prior = base_weights.T.astype(jnp.float32) - (0.567 / 8192.0) * known.T.astype(jnp.float32)
    with jax.named_scope("sketch_y"):
        half = spread(sketch, "y", 4)
        half, prior = lax.optimization_barrier((half, prior))
        half = jnp.concatenate(halves(half.reshape(width // 2, rank)), axis=1)
    with jax.named_scope("sketch_core"):
        half_other = swap(half, "core")
    with jax.named_scope("decode"):
        here = lax.axis_index("core") * (width // 2)
        there = width // 2 - here
        twice = jnp.concatenate([gauss, gauss], axis=1)
        own_twice = jnp.concatenate([sketch_matrix, sketch_matrix], axis=1)
        turned = jnp.zeros((width, held), jnp.bfloat16)
        rows_own = []
        for part, start in ((half, here), (half_other, there)):
            decoded = lax.dot_general(part, twice, CONTRACT, preferred_element_type=jnp.float32)
            piece = lax.dynamic_slice_in_dim(prior, start, width // 2, 0) - 1.33 * decoded
            turned = lax.dynamic_update_slice_in_dim(turned, piece.astype(jnp.bfloat16), start, 0)
            rows_own.append(lax.dot_general(own_twice, part, CONTRACT, preferred_element_type=jnp.float32))
        new_weights = turned.T
    with jax.named_scope("new_momentum"):
        first = lax.axis_index("core") == 0
        left, right = jnp.where(first, rows_own[0], rows_own[1]), jnp.where(first, rows_own[1], rows_own[0])
        new_momentum = 0.9 * momentum + jnp.concatenate([left, right], axis=1)
    return new_weights, new_momentum


def solution(mesh):
    fine = Mesh(mesh.devices.reshape(SIZES), ALL)
    placed = (P(FSDP, None), P(REP, FSDP, None), P(FSDP + REP, None), P(FSDP + REP, None))
    return jax.shard_map(
        shards,
        mesh=fine,
        in_specs=placed,
        out_specs=(P(FSDP, None), P(FSDP + REP, None)),
        check_vma=False,
    )
```

time: 141 us -> 136 us (0.965)
  waiting for transfers between devices: 33.6 us -> 18.5 us
  blocking collectives: 17.6 us -> 31.2 us
  starting transfers between devices: 72.4 us -> 63.5 us
  matrix products: 2.47 us -> 4.98 us
  local copies, waits for them, and re-layouts: 5.43 us -> 7.74 us
    all_to_all x0 -> x1, blocking collectives: none -> 16.3 us  [shards(): lax.all_to_all(padded.reshape(16, 8, rank), NEAR, 0, 0, tiled=True)]
    all_to_all x3 -> x1, starting transfers between devices: 22.3 us -> 10.5 us  [shards(): lax.all_to_all(local_weights[0].T.reshape(CUTS, cols, held), CUT, 0, 0, t...]
    all_to_all x3 -> x1, waiting for transfers between devices: 9.27 us -> 0.01 us  [shards(): lax.all_to_all(local_weights[0].T.reshape(CUTS, cols, held), CUT, 0, 0, t...]
    ppermute x0 -> x3, starting transfers between devices: none -> 8.41 us  [around_y(): lax.ppermute(value, ALL, [(int(a), int(b)) for a, b in zip(index.ravel(),...]
    sub x0 -> x1, other arithmetic: none -> 4.11 us  [shards(): base_weights.T.astype(jnp.float32)]
    all_to_all x2 -> x3, waiting for transfers between devices: 20.4 us -> 16.4 us  [spread(): lax.all_to_all(jnp.broadcast_to(value[None], (parts,) + value.shape), axe...]
    concatenate x3 -> x1, other arithmetic: 4.02 us -> 0.11 us  [shards(): half = jnp.concatenate(halves(half.reshape(width // 2, rank)), axis=1)]
    all_to_all x2 -> x3, starting transfers between devices: 15.8 us -> 12.5 us  [spread(): lax.all_to_all(jnp.broadcast_to(value[None], (parts,) + value.shape), axe...]
  transfers between devices with their start and end apart: 8 -> 11, of which waited for: 5 -> 4; matrix products, arithmetic and copies ran while one was open for 2% -> 11% of each run, Pallas kernels for 0% -> 0%
where the time goes in v3:
time: 136 us
  starting transfers between devices  63.5 us (47%)
  blocking collectives  31.2 us (23%)
  waiting for transfers between devices  18.5 us (14%)
  other arithmetic  8.52 us (6%)
  local copies, waits for them, and re-layouts  7.74 us (6%)
  matrix products  4.98 us (4%)
    ppermute x4, starting transfers between devices, swap(): return lax.ppermute(value, ALL, swapped(axis))  32 us
    all_to_all x3, waiting for transfers between devices, spread(): lax.all_to_all(jnp.broadcast_to(value[None], (parts,) + value.shape), axe...  16.4 us
    all_to_all x1, blocking collectives, shards(): lax.all_to_all(padded.reshape(16, 8, rank), NEAR, 0, 0, tiled=True)  16.3 us
    all_gather x1, blocking collectives, shards(): lax.all_gather(sketch_pair.reshape(2 * rows, rank), PLANE, axis=0, tiled=...  14.9 us
    all_to_all x3, starting transfers between devices, spread(): lax.all_to_all(jnp.broadcast_to(value[None], (parts,) + value.shape), axe...  12.5 us
    all_to_all x1, starting transfers between devices, shards(): lax.all_to_all(local_weights[0].T.reshape(CUTS, cols, held), CUT, 0, 0, t...  10.5 us
    ppermute x3, starting transfers between devices, around_y(): lax.ppermute(value, ALL, [(int(a), int(b)) for a, b in zip(index.ravel(),...  8.41 us
    sub x1, other arithmetic, shards(): base_weights.T.astype(jnp.float32)  4.11 us
  transfers between devices with their start and end apart: 11, of which 4 were waited for; matrix products, arithmetic and copies ran while one was open for 11% of the time, Pallas kernels for 0%

profile of v3, /device:TPU:1, one launch (start us, length us, event | category | flops | bytes accessed | tf_op | source)
XLA Modules:
  0.0 135.5 jit_solution(12197967721159759701)
XLA Ops:
  0.6 10.5 %all-to-all-start = ((bf16[8,104,896]{2,1,0:T(8,128)(2,1)}), bf16[8,104,896]{2,1,0:T(8,128)(2,1)S(1)}, u32[]{:S(2)}, u32[]{:S(2)}) async-start(bf16[8,104,896]{2,1,0:T(8,128)(2,1)} %bitcast.74), calls=%async_computation | async-start | bytes 2981888 | tf_op jit(solution)/shard_map/local_columns/all_to_all | solution.py:72
  11.2 11.0 %collective-permute-start = (bf16[56,512]{1,0:T(8,128)(2,1)S(1)}, bf16[56,512]{1,0:T(8,128)(2,1)S(1)}, u32[]{:S(2)}, u32[]{:S(2)}) collective-permute-start(bf16[56,512]{1,0:T(8,128)(2,1)S(1)} %copy-done.5), channel_id=1, source_target_pairs={{0,256},{1,257},{2,258},{3,259},{4,260},{5,261},{6,262},{7,263},{8... | collective-permute-start | bytes 172040 | tf_op jit(solution)/shard_map/sketch_rows_zhi/ppermute | solution.py:28
  23.2 2.1 %collective-permute-done = bf16[56,512]{1,0:T(8,128)(2,1)S(1)} collective-permute-done((bf16[56,512]{1,0:T(8,128)(2,1)S(1)}, bf16[56,512]{1,0:T(8,128)(2,1)S(1)}, u32[]{:S(2)}, u32[]{:S(2)}) %collective-permute-start) | collective-permute-done | bytes 57376 | tf_op jit(solution)/shard_map/sketch_rows_zhi/ppermute | solution.py:28
  25.3 14.9 %all_gather.3 = bf16[8,112,512]{2,1,0:T(8,128)(2,1)S(1)} all-gather(bf16[1,112,512]{2,1,0:T(8,128)(2,1)S(1)} %bitcast.76), channel_id=1, replica_groups=mesh['zhi'=2,'y'=4,'core'=2,'zm'=2,'zn'=4,'x'=4] {'y','core'}, dimensions={0}, use_global_device_ids=true | all-gather | bytes 1032192 | tf_op jit(solution)/shard_map/sketch_rows_plane/all_gather | solution.py:74
  41.2 16.3 %all_to_all.25 = f32[16,8,512]{2,1,0:T(8,128)S(1)} all-to-all(f32[16,8,512]{2,1,0:T(8,128)S(1)} %pad_bitcast_fusion), channel_id=1, replica_groups=mesh['zhi'=2,'y'=4,'core'=2,'zm'=2,'zn'=4,'x'=4] {'zn','x'}, dimensions={0} | all-to-all | bytes 524288 | tf_op jit(solution)/shard_map/sketch_sum/all_to_all | solution.py:83
  57.6 12.9 %collective-permute-start.1 = (f16[56,832]{1,0:T(8,128)(2,1)S(1)}, f16[56,832]{1,0:T(8,128)(2,1)S(1)}, u32[]{:S(2)}, u32[]{:S(2)}) collective-permute-start(f16[56,832]{1,0:T(8,128)(2,1)S(1)} %multiply_convert_fusion), channel_id=1, source_target_pairs={{0,256},{1,257},{2,258},{3,259},{4,260},{5,261},{6,262},{7,263},{8... | collective-permute-start | bytes 279560 | tf_op jit(solution)/shard_map/sketch_sum/ppermute | solution.py:28
  71.2 3.3 %all-to-all-start.2 = ((f32[4,8,512]{2,1,0:T(8,128)}), f32[4,8,512]{2,1,0:T(8,128)S(1)}, u32[]{:S(2)}, u32[]{:S(2)}) async-start(f32[4,8,512]{2,1,0:T(8,128)} %broadcast_in_dim.9), calls=%async_computation.2 | async-start | bytes 131072 | tf_op jit(solution)/shard_map/sketch_sum/all_to_all | solution.py:46
  74.6 4.0 %collective-permute-start.2 = (f16[112,832]{1,0:T(8,128)(2,1)S(1)}, f16[112,832]{1,0:T(8,128)(2,1)S(1)}, u32[]{:S(2)}, u32[]{:S(2)}) collective-permute-start(f16[112,832]{1,0:T(8,128)(2,1)S(1)} %bitcast.69), channel_id=1, source_target_pairs={{0,192},{1,193},{2,194},{3,195},{4,196},{5,197},{6,198},{7,199},{8... | collective-permute-start | bytes 559112 | tf_op jit(solution)/shard_map/sketch_sum/ppermute | solution.py:36
  78.6 2.5 %collective-permute-start.3 = (f16[112,832]{1,0:T(8,128)(2,1)S(1)}, f16[112,832]{1,0:T(8,128)(2,1)S(1)}, u32[]{:S(2)}, u32[]{:S(2)}) collective-permute-start(f16[112,832]{1,0:T(8,128)(2,1)S(1)} %bitcast.70), channel_id=1, source_target_pairs={{0,128},{1,129},{2,130},{3,131},{4,132},{5,133},{6,134},{7,135},{8... | collective-permute-start | bytes 559112 | tf_op jit(solution)/shard_map/sketch_sum/ppermute | solution.py:36
  81.1 1.9 %collective-permute-start.4 = (f16[112,832]{1,0:T(8,128)(2,1)S(1)}, f16[112,832]{1,0:T(8,128)(2,1)S(1)}, u32[]{:S(2)}, u32[]{:S(2)}) collective-permute-start(f16[112,832]{1,0:T(8,128)(2,1)S(1)} %bitcast.71), channel_id=1, source_target_pairs={{0,64},{1,65},{2,66},{3,67},{4,68},{5,69},{6,70},{7,71},{8,72},{9,... | collective-permute-start | bytes 559112 | tf_op jit(solution)/shard_map/sketch_sum/ppermute | solution.py:36
  83.0 3.4 %all-to-all-done.2 = f32[4,8,512]{2,1,0:T(8,128)S(1)} async-done(((f32[4,8,512]{2,1,0:T(8,128)}), f32[4,8,512]{2,1,0:T(8,128)S(1)}, u32[]{:S(2)}, u32[]{:S(2)}) %all-to-all-start.2) | async-done | bytes 65568 | tf_op jit(solution)/shard_map/sketch_sum/all_to_all | solution.py:46
  87.2 5.1 %all-to-all-start.3 = ((f32[16,8,512]{2,1,0:T(8,128)}), f32[16,8,512]{2,1,0:T(8,128)S(1)}, u32[]{:S(2)}, u32[]{:S(2)}) async-start(f32[16,8,512]{2,1,0:T(8,128)} %broadcast_in_dim.10), calls=%async_computation.3 | async-start | bytes 524288 | tf_op jit(solution)/shard_map/sketch_sum/all_to_all | solution.py:46
  92.8 8.3 %all-to-all-done.3 = f32[16,8,512]{2,1,0:T(8,128)S(1)} async-done(((f32[16,8,512]{2,1,0:T(8,128)}), f32[16,8,512]{2,1,0:T(8,128)S(1)}, u32[]{:S(2)}, u32[]{:S(2)}) %all-to-all-start.3) | async-done | bytes 262176 | tf_op jit(solution)/shard_map/sketch_sum/all_to_all | solution.py:46
  101.1 4.9 %collective-permute-start.5 = (f16[4,112,832]{2,1,0:T(8,128)(2,1)S(1)}, f16[4,112,832]{2,1,0:T(8,128)(2,1)S(1)}, u32[]{:S(2)}, u32[]{:S(2)}) collective-permute-start(f16[4,112,832]{2,1,0:T(8,128)(2,1)S(1)} %constant_dynamic-slice_fusion), channel_id=1, source_target_pairs={{0,32},{1,33},{2,34},{3,35},{4,36},{5,37},{6,38},{7,39},{8,40},{9,... | collective-permute-start | bytes 2236424 | tf_op jit(solution)/shard_map/momentum_core/ppermute | solution.py:28
  106.0 1.0 broadcast_in_dim.11
  107.0 4.2 %all-to-all-start.4 = ((f32[4,104,512]{2,1,0:T(8,128)}), f32[4,104,512]{2,1,0:T(8,128)}, u32[]{:S(2)}, u32[]{:S(2)}) async-start(f32[4,104,512]{2,1,0:T(8,128)} %broadcast_in_dim.11), calls=%async_computation.4 | async-start | bytes 1703936 | tf_op jit(solution)/shard_map/sketch_y/all_to_all | solution.py:46
  112.3 3.0 %copy.20 = f32[896,832]{0,1:T(8,128)} copy(f32[896,832]{1,0:T(8,128)S(1)} %bitcast.64) | data formatting | bytes 5963776 | tf_op jit(solution)/shard_map/prior/mul | solution.py:95
  115.3 4.1 %subtract_bitcast_fusion = f32[832,896]{1,0:T(8,128)} fusion(f32[896,832]{0,1:T(8,128)} %copy.20, bf16[896,832]{0,1:T(8,128)(2,1)} %param.4), kind=kLoop, calls=%fused_computation.1 | loop fusion | flops 1490944 | bytes 7454720 | tf_op jit(solution)/shard_map/prior/sub | solution.py:95
  119.4 4.8 %all-to-all-done.4 = f32[4,104,512]{2,1,0:T(8,128)} async-done(((f32[4,104,512]{2,1,0:T(8,128)}), f32[4,104,512]{2,1,0:T(8,128)}, u32[]{:S(2)}, u32[]{:S(2)}) %all-to-all-start.4) | async-done | bytes 852000 | tf_op jit(solution)/shard_map/sketch_y/all_to_all | solution.py:46
  124.2 1.3 reduce-precision_convert_fusion
  125.6 3.2 %collective-permute-start.6 = (bf16[416,1024]{1,0:T(8,128)(2,1)S(1)}, bf16[416,1024]{1,0:T(8,128)(2,1)S(1)}, u32[]{:S(2)}, u32[]{:S(2)}) collective-permute-start(bf16[416,1024]{1,0:T(8,128)(2,1)S(1)} %pad_maximum_fusion.11), channel_id=1, source_target_pairs={{0,32},{1,33},{2,34},{3,35},{4,36},{5,37},{6,38},{7,39},{8,40},{9,... | collective-permute-start | bytes 2555912 | tf_op jit(solution)/shard_map/sketch_core/ppermute | solution.py:28
  128.9 2.5 %fusion.2 = bf16[832,896]{1,0:T(8,128)(2,1)S(1)} fusion(bf16[832,896]{1,0:T(8,128)(2,1)S(1)} %broadcast_in_dim.8, s32[]{:T(128)S(6)} %select_n.84, bf16[416,1024]{1,0:T(8,128)(2,1)S(1)} %pad_maximum_fusion.11, bf16[896,512]{1,0:T(8,128)(2,1)S(1)} %bitcast.66, f32[832,896]{1,0:T(8,128)} %subtract_bitcast_fusion), kind=kOutput, calls=%fused_computation.8 | convolution fusion | flops 768151552 | bytes 4005892 | tf_op jit(solution)/shard_map/decode/dot_general | solution.py:110
  133.3 1.1 fusion.3
  134.4 1.1 copy-done.4
  (51 shorter events, 7.0 us)
Async XLA Ops:
  0.6 10.5 %copy-start.5 = (bf16[56,512]{1,0:T(8,128)(2,1)S(1)}, bf16[56,512]{1,0:T(8,128)(2,1)}, u32[]{:S(2)}) copy-start(bf16[56,512]{1,0:T(8,128)(2,1)} %param.7) | copy-start | bytes 172036
  0.6 39.6 %all-to-all-start = ((bf16[8,104,896]{2,1,0:T(8,128)(2,1)}), bf16[8,104,896]{2,1,0:T(8,128)(2,1)S(1)}, u32[]{:S(2)}, u32[]{:S(2)}) async-start(bf16[8,104,896]{2,1,0:T(8,128)(2,1)} %bitcast.74), calls=%async_computation | async-start | bytes 2981888 | tf_op jit(solution)/shard_map/local_columns/all_to_all | solution.py:72
  11.2 14.1 %collective-permute-start = (bf16[56,512]{1,0:T(8,128)(2,1)S(1)}, bf16[56,512]{1,0:T(8,128)(2,1)S(1)}, u32[]{:S(2)}, u32[]{:S(2)}) collective-permute-start(bf16[56,512]{1,0:T(8,128)(2,1)S(1)} %copy-done.5), channel_id=1, source_target_pairs={{0,256},{1,257},{2,258},{3,259},{4,260},{5,261},{6,262},{7,263},{8... | collective-permute-start | bytes 172040 | tf_op jit(solution)/shard_map/sketch_rows_zhi/ppermute | solution.py:28
  40.3 0.9 copy-start
  40.6 17.0 %copy-start.3 = (f32[56,832]{1,0:T(8,128)S(1)}, f32[56,832]{1,0:T(8,128)}, u32[]{:S(2)}) copy-start(f32[56,832]{1,0:T(8,128)} %param.6) | copy-start | bytes 559108
  57.6 16.8 %collective-permute-start.1 = (f16[56,832]{1,0:T(8,128)(2,1)S(1)}, f16[56,832]{1,0:T(8,128)(2,1)S(1)}, u32[]{:S(2)}, u32[]{:S(2)}) collective-permute-start(f16[56,832]{1,0:T(8,128)(2,1)S(1)} %multiply_convert_fusion), channel_id=1, source_target_pairs={{0,256},{1,257},{2,258},{3,259},{4,260},{5,261},{6,262},{7,263},{8... | collective-permute-start | bytes 279560 | tf_op jit(solution)/shard_map/sketch_sum/ppermute | solution.py:28
  71.2 15.3 %all-to-all-start.2 = ((f32[4,8,512]{2,1,0:T(8,128)}), f32[4,8,512]{2,1,0:T(8,128)S(1)}, u32[]{:S(2)}, u32[]{:S(2)}) async-start(f32[4,8,512]{2,1,0:T(8,128)} %broadcast_in_dim.9), calls=%async_computation.2 | async-start | bytes 131072 | tf_op jit(solution)/shard_map/sketch_sum/all_to_all | solution.py:46
  74.6 17.7 %collective-permute-start.2 = (f16[112,832]{1,0:T(8,128)(2,1)S(1)}, f16[112,832]{1,0:T(8,128)(2,1)S(1)}, u32[]{:S(2)}, u32[]{:S(2)}) collective-permute-start(f16[112,832]{1,0:T(8,128)(2,1)S(1)} %bitcast.69), channel_id=1, source_target_pairs={{0,192},{1,193},{2,194},{3,195},{4,196},{5,197},{6,198},{7,199},{8... | collective-permute-start | bytes 559112 | tf_op jit(solution)/shard_map/sketch_sum/ppermute | solution.py:36
  78.6 13.7 %collective-permute-start.3 = (f16[112,832]{1,0:T(8,128)(2,1)S(1)}, f16[112,832]{1,0:T(8,128)(2,1)S(1)}, u32[]{:S(2)}, u32[]{:S(2)}) collective-permute-start(f16[112,832]{1,0:T(8,128)(2,1)S(1)} %bitcast.70), channel_id=1, source_target_pairs={{0,128},{1,129},{2,130},{3,131},{4,132},{5,133},{6,134},{7,135},{8... | collective-permute-start | bytes 559112 | tf_op jit(solution)/shard_map/sketch_sum/ppermute | solution.py:36
  81.1 11.3 %collective-permute-start.4 = (f16[112,832]{1,0:T(8,128)(2,1)S(1)}, f16[112,832]{1,0:T(8,128)(2,1)S(1)}, u32[]{:S(2)}, u32[]{:S(2)}) collective-permute-start(f16[112,832]{1,0:T(8,128)(2,1)S(1)} %bitcast.71), channel_id=1, source_target_pairs={{0,64},{1,65},{2,66},{3,67},{4,68},{5,69},{6,70},{7,71},{8,72},{9,... | collective-permute-start | bytes 559112 | tf_op jit(solution)/shard_map/sketch_sum/ppermute | solution.py:36
  87.2 13.9 %all-to-all-start.3 = ((f32[16,8,512]{2,1,0:T(8,128)}), f32[16,8,512]{2,1,0:T(8,128)S(1)}, u32[]{:S(2)}, u32[]{:S(2)}) async-start(f32[16,8,512]{2,1,0:T(8,128)} %broadcast_in_dim.10), calls=%async_computation.3 | async-start | bytes 524288 | tf_op jit(solution)/shard_map/sketch_sum/all_to_all | solution.py:46
  101.1 10.2 %collective-permute-start.5 = (f16[4,112,832]{2,1,0:T(8,128)(2,1)S(1)}, f16[4,112,832]{2,1,0:T(8,128)(2,1)S(1)}, u32[]{:S(2)}, u32[]{:S(2)}) collective-permute-start(f16[4,112,832]{2,1,0:T(8,128)(2,1)S(1)} %constant_dynamic-slice_fusion), channel_id=1, source_target_pairs={{0,32},{1,33},{2,34},{3,35},{4,36},{5,37},{6,38},{7,39},{8,40},{9,... | collective-permute-start | bytes 2236424 | tf_op jit(solution)/shard_map/momentum_core/ppermute | solution.py:28
  107.0 17.1 %all-to-all-start.4 = ((f32[4,104,512]{2,1,0:T(8,128)}), f32[4,104,512]{2,1,0:T(8,128)}, u32[]{:S(2)}, u32[]{:S(2)}) async-start(f32[4,104,512]{2,1,0:T(8,128)} %broadcast_in_dim.11), calls=%async_computation.4 | async-start | bytes 1703936 | tf_op jit(solution)/shard_map/sketch_y/all_to_all | solution.py:46
  125.5 3.4 %copy-start.1 = (bf16[2,8,56,512]{3,2,1,0:T(8,128)(2,1)S(1)}, bf16[2,8,56,512]{3,2,1,0:T(8,128)(2,1)}, u32[]{:S(2)}) copy-start(bf16[2,8,56,512]{3,2,1,0:T(8,128)(2,1)} %copy-done) | copy-start | bytes 2752516
  125.6 5.8 %collective-permute-start.6 = (bf16[416,1024]{1,0:T(8,128)(2,1)S(1)}, bf16[416,1024]{1,0:T(8,128)(2,1)S(1)}, u32[]{:S(2)}, u32[]{:S(2)}) collective-permute-start(bf16[416,1024]{1,0:T(8,128)(2,1)S(1)} %pad_maximum_fusion.11), channel_id=1, source_target_pairs={{0,32},{1,33},{2,34},{3,35},{4,36},{5,37},{6,38},{7,39},{8,40},{9,... | collective-permute-start | bytes 2555912 | tf_op jit(solution)/shard_map/sketch_core/ppermute | solution.py:28
  131.4 1.8 %copy-start.2 = (f32[832,896]{1,0:T(8,128)S(1)}, f32[832,896]{1,0:T(8,128)}, u32[]{:S(2)}) copy-start(f32[832,896]{1,0:T(8,128)} %subtract_bitcast_fusion) | copy-start | bytes 8945668
  134.4 1.1 copy-start.4

commit v4 on v3

--- a/solution.py
+++ b/solution.py
@@ -87,16 +87,19 @@
         momentum_y = around_y(momentum_pair.reshape(2 * rows, width))
         mine = jnp.sum(spread(mine, FAR, 4), axis=0)
         sketch = spread(mine, NEAR, 16).reshape(128, rank)[:cols] / GROUPS
-    sketch, momentum_y = lax.optimization_barrier((sketch, momentum_y))
+    with jax.named_scope("sketch_y"):
+        copies = jnp.concatenate(halves(sketch), axis=1)
+        copies = jnp.broadcast_to(copies[None], (4,) + copies.shape)
+        copies, momentum_y = lax.optimization_barrier((copies, momentum_y))
     with jax.named_scope("momentum_core"):
         momentum_all = in_order(momentum_y, swap(momentum_y, "core"), "core", 1)
     with jax.named_scope("prior"):
         known = momentum_all.reshape(CUTS, 2, rows, width).transpose(1, 0, 2, 3).reshape(held, width)
         prior = base_weights.T.astype(jnp.float32) - (0.567 / 8192.0) * known.T.astype(jnp.float32)
     with jax.named_scope("sketch_y"):
-        half = spread(sketch, "y", 4)
+        half = lax.all_to_all(copies, "y", 0, 0, tiled=True)
         half, prior = lax.optimization_barrier((half, prior))
-        half = jnp.concatenate(halves(half.reshape(width // 2, rank)), axis=1)
+        half = half.reshape(width // 2, 2 * rank)
     with jax.named_scope("sketch_core"):
         half_other = swap(half, "core")
     with jax.named_scope("decode"):
@@ -113,6 +116,7 @@
             rows_own.append(lax.dot_general(own_twice, part, CONTRACT, preferred_element_type=jnp.float32))
         new_weights = turned.T
     with jax.named_scope("new_momentum"):
+        rows_own = lax.optimization_barrier(rows_own)
         first = lax.axis_index("core") == 0
         left, right = jnp.where(first, rows_own[0], rows_own[1]), jnp.where(first, rows_own[1], rows_own[0])
         new_momentum = 0.9 * momentum + jnp.concatenate([left, right], axis=1)

time: 136 us -> 136 us (level)
  matrix products: 4.98 us -> 6.55 us
    all_to_all x3 -> x2, waiting for transfers between devices: 16.4 us -> 11.7 us  [spread(): lax.all_to_all(jnp.broadcast_to(value[None], (parts,) + value.shape), axe...]
    all_to_all x0 -> x1, waiting for transfers between devices: none -> 4.76 us  [shards(): half = lax.all_to_all(copies, 'y', 0, 0, tiled=True)]
    all_to_all x0 -> x1, starting transfers between devices: none -> 4.22 us  [shards(): half = lax.all_to_all(copies, 'y', 0, 0, tiled=True)]
    all_to_all x3 -> x2, starting transfers between devices: 12.5 us -> 8.34 us  [spread(): lax.all_to_all(jnp.broadcast_to(value[None], (parts,) + value.shape), axe...]
  transfers between devices with their start and end apart: 11 -> 11, of which waited for: 4 -> 4; matrix products, arithmetic and copies ran while one was open for 11% -> 12% of each run, Pallas kernels for 0% -> 0%
where the time goes in v4:
time: 136 us; the launch traced here: 135 us
  starting transfers between devices  63.3 us (47%)
  blocking collectives  31.2 us (23%)
  waiting for transfers between devices  18.5 us (14%)
  local copies, waits for them, and re-layouts  7.46 us (5%)
  other arithmetic  7.18 us (5%)
  matrix products  6.55 us (5%)
    ppermute x4, starting transfers between devices, swap(): return lax.ppermute(value, ALL, swapped(axis))  31.8 us
    all_to_all x1, blocking collectives, shards(): lax.all_to_all(padded.reshape(16, 8, rank), NEAR, 0, 0, tiled=True)  16.3 us
    all_gather x1, blocking collectives, shards(): lax.all_gather(sketch_pair.reshape(2 * rows, rank), PLANE, axis=0, tiled=...  14.9 us
    all_to_all x2, waiting for transfers between devices, spread(): lax.all_to_all(jnp.broadcast_to(value[None], (parts,) + value.shape), axe...  11.7 us
    all_to_all x1, starting transfers between devices, shards(): lax.all_to_all(local_weights[0].T.reshape(CUTS, cols, held), CUT, 0, 0, t...  10.5 us
    ppermute x3, starting transfers between devices, around_y(): lax.ppermute(value, ALL, [(int(a), int(b)) for a, b in zip(index.ravel(),...  8.41 us
    all_to_all x2, starting transfers between devices, spread(): lax.all_to_all(jnp.broadcast_to(value[None], (parts,) + value.shape), axe...  8.34 us
    all_to_all x1, waiting for transfers between devices, shards(): half = lax.all_to_all(copies, 'y', 0, 0, tiled=True)  4.76 us
  transfers between devices with their start and end apart: 11, of which 4 were waited for; matrix products, arithmetic and copies ran while one was open for 12% of the time, Pallas kernels for 0%

profile of v4, /device:TPU:1, one launch (start us, length us, event | category | flops | bytes accessed | tf_op | source)
XLA Modules:
  0.0 135.3 jit_solution(109562003847007455)
XLA Ops:
  0.6 10.5 %all-to-all-start = ((bf16[8,104,896]{2,1,0:T(8,128)(2,1)}), bf16[8,104,896]{2,1,0:T(8,128)(2,1)S(1)}, u32[]{:S(2)}, u32[]{:S(2)}) async-start(bf16[8,104,896]{2,1,0:T(8,128)(2,1)} %bitcast.76), calls=%async_computation | async-start | bytes 2981888 | tf_op jit(solution)/shard_map/local_columns/all_to_all | solution.py:72
  11.2 11.0 %collective-permute-start = (bf16[56,512]{1,0:T(8,128)(2,1)S(1)}, bf16[56,512]{1,0:T(8,128)(2,1)S(1)}, u32[]{:S(2)}, u32[]{:S(2)}) collective-permute-start(bf16[56,512]{1,0:T(8,128)(2,1)S(1)} %copy-done.5), channel_id=1, source_target_pairs={{0,256},{1,257},{2,258},{3,259},{4,260},{5,261},{6,262},{7,263},{8... | collective-permute-start | bytes 172040 | tf_op jit(solution)/shard_map/sketch_rows_zhi/ppermute | solution.py:28
  23.2 2.1 %collective-permute-done = bf16[56,512]{1,0:T(8,128)(2,1)S(1)} collective-permute-done((bf16[56,512]{1,0:T(8,128)(2,1)S(1)}, bf16[56,512]{1,0:T(8,128)(2,1)S(1)}, u32[]{:S(2)}, u32[]{:S(2)}) %collective-permute-start) | collective-permute-done | bytes 57376 | tf_op jit(solution)/shard_map/sketch_rows_zhi/ppermute | solution.py:28
  25.3 14.9 %all_gather.3 = bf16[8,112,512]{2,1,0:T(8,128)(2,1)S(1)} all-gather(bf16[1,112,512]{2,1,0:T(8,128)(2,1)S(1)} %bitcast.78), channel_id=1, replica_groups=mesh['zhi'=2,'y'=4,'core'=2,'zm'=2,'zn'=4,'x'=4] {'y','core'}, dimensions={0}, use_global_device_ids=true | all-gather | bytes 1032192 | tf_op jit(solution)/shard_map/sketch_rows_plane/all_gather | solution.py:74
  41.2 16.3 %all_to_all.25 = f32[16,8,512]{2,1,0:T(8,128)S(1)} all-to-all(f32[16,8,512]{2,1,0:T(8,128)S(1)} %pad_bitcast_fusion), channel_id=1, replica_groups=mesh['zhi'=2,'y'=4,'core'=2,'zm'=2,'zn'=4,'x'=4] {'zn','x'}, dimensions={0} | all-to-all | bytes 524288 | tf_op jit(solution)/shard_map/sketch_sum/all_to_all | solution.py:83
  57.6 12.9 %collective-permute-start.1 = (f16[56,832]{1,0:T(8,128)(2,1)S(1)}, f16[56,832]{1,0:T(8,128)(2,1)S(1)}, u32[]{:S(2)}, u32[]{:S(2)}) collective-permute-start(f16[56,832]{1,0:T(8,128)(2,1)S(1)} %multiply_convert_fusion), channel_id=1, source_target_pairs={{0,256},{1,257},{2,258},{3,259},{4,260},{5,261},{6,262},{7,263},{8... | collective-permute-start | bytes 279560 | tf_op jit(solution)/shard_map/sketch_sum/ppermute | solution.py:28
  71.2 3.3 %all-to-all-start.2 = ((f32[4,8,512]{2,1,0:T(8,128)}), f32[4,8,512]{2,1,0:T(8,128)S(1)}, u32[]{:S(2)}, u32[]{:S(2)}) async-start(f32[4,8,512]{2,1,0:T(8,128)} %broadcast_in_dim.9), calls=%async_computation.2 | async-start | bytes 131072 | tf_op jit(solution)/shard_map/sketch_sum/all_to_all | solution.py:46
  74.6 4.0 %collective-permute-start.2 = (f16[112,832]{1,0:T(8,128)(2,1)S(1)}, f16[112,832]{1,0:T(8,128)(2,1)S(1)}, u32[]{:S(2)}, u32[]{:S(2)}) collective-permute-start(f16[112,832]{1,0:T(8,128)(2,1)S(1)} %bitcast.71), channel_id=1, source_target_pairs={{0,192},{1,193},{2,194},{3,195},{4,196},{5,197},{6,198},{7,199},{8... | collective-permute-start | bytes 559112 | tf_op jit(solution)/shard_map/sketch_sum/ppermute | solution.py:36
  78.6 2.5 %collective-permute-start.3 = (f16[112,832]{1,0:T(8,128)(2,1)S(1)}, f16[112,832]{1,0:T(8,128)(2,1)S(1)}, u32[]{:S(2)}, u32[]{:S(2)}) collective-permute-start(f16[112,832]{1,0:T(8,128)(2,1)S(1)} %bitcast.72), channel_id=1, source_target_pairs={{0,128},{1,129},{2,130},{3,131},{4,132},{5,133},{6,134},{7,135},{8... | collective-permute-start | bytes 559112 | tf_op jit(solution)/shard_map/sketch_sum/ppermute | solution.py:36
  81.1 1.9 %collective-permute-start.4 = (f16[112,832]{1,0:T(8,128)(2,1)S(1)}, f16[112,832]{1,0:T(8,128)(2,1)S(1)}, u32[]{:S(2)}, u32[]{:S(2)}) collective-permute-start(f16[112,832]{1,0:T(8,128)(2,1)S(1)} %bitcast.73), channel_id=1, source_target_pairs={{0,64},{1,65},{2,66},{3,67},{4,68},{5,69},{6,70},{7,71},{8,72},{9,... | collective-permute-start | bytes 559112 | tf_op jit(solution)/shard_map/sketch_sum/ppermute | solution.py:36
  83.0 3.4 %all-to-all-done.2 = f32[4,8,512]{2,1,0:T(8,128)S(1)} async-done(((f32[4,8,512]{2,1,0:T(8,128)}), f32[4,8,512]{2,1,0:T(8,128)S(1)}, u32[]{:S(2)}, u32[]{:S(2)}) %all-to-all-start.2) | async-done | bytes 65568 | tf_op jit(solution)/shard_map/sketch_sum/all_to_all | solution.py:46
  87.2 5.1 %all-to-all-start.3 = ((f32[16,8,512]{2,1,0:T(8,128)}), f32[16,8,512]{2,1,0:T(8,128)S(1)}, u32[]{:S(2)}, u32[]{:S(2)}) async-start(f32[16,8,512]{2,1,0:T(8,128)} %broadcast_in_dim.10), calls=%async_computation.3 | async-start | bytes 524288 | tf_op jit(solution)/shard_map/sketch_sum/all_to_all | solution.py:46
  92.8 8.3 %all-to-all-done.3 = f32[16,8,512]{2,1,0:T(8,128)S(1)} async-done(((f32[16,8,512]{2,1,0:T(8,128)}), f32[16,8,512]{2,1,0:T(8,128)S(1)}, u32[]{:S(2)}, u32[]{:S(2)}) %all-to-all-start.3) | async-done | bytes 262176 | tf_op jit(solution)/shard_map/sketch_sum/all_to_all | solution.py:46
  101.1 1.0 broadcast_in_dim.11
  102.1 4.9 %collective-permute-start.5 = (f16[4,112,832]{2,1,0:T(8,128)(2,1)S(1)}, f16[4,112,832]{2,1,0:T(8,128)(2,1)S(1)}, u32[]{:S(2)}, u32[]{:S(2)}) collective-permute-start(f16[4,112,832]{2,1,0:T(8,128)(2,1)S(1)} %constant_dynamic-slice_fusion), channel_id=1, source_target_pairs={{0,32},{1,33},{2,34},{3,35},{4,36},{5,37},{6,38},{7,39},{8,40},{9,... | collective-permute-start | bytes 2236424 | tf_op jit(solution)/shard_map/momentum_core/ppermute | solution.py:28
  107.1 4.2 %all-to-all-start.4 = ((bf16[4,104,1024]{2,1,0:T(8,128)(2,1)}), bf16[4,104,1024]{2,1,0:T(8,128)(2,1)}, u32[]{:S(2)}, u32[]{:S(2)}) async-start(bf16[4,104,1024]{2,1,0:T(8,128)(2,1)} %broadcast_in_dim.11), calls=%async_computation.4 | async-start | bytes 1703936 | tf_op jit(solution)/shard_map/sketch_y/all_to_all | solution.py:100
  112.3 3.0 %copy.20 = f32[896,832]{0,1:T(8,128)} copy(f32[896,832]{1,0:T(8,128)S(1)} %bitcast.66) | data formatting | bytes 5963776 | tf_op jit(solution)/shard_map/prior/mul | solution.py:98
  115.3 4.1 %subtract_bitcast_fusion = f32[832,896]{1,0:T(8,128)} fusion(f32[896,832]{0,1:T(8,128)} %copy.20, bf16[896,832]{0,1:T(8,128)(2,1)} %param.4), kind=kLoop, calls=%fused_computation.1 | loop fusion | flops 1490944 | bytes 7454720 | tf_op jit(solution)/shard_map/prior/sub | solution.py:98
  119.5 4.8 %all-to-all-done.4 = bf16[4,104,1024]{2,1,0:T(8,128)(2,1)} async-done(((bf16[4,104,1024]{2,1,0:T(8,128)(2,1)}), bf16[4,104,1024]{2,1,0:T(8,128)(2,1)}, u32[]{:S(2)}, u32[]{:S(2)}) %all-to-all-start.4) | async-done | bytes 852000 | tf_op jit(solution)/shard_map/sketch_y/all_to_all | solution.py:100
  124.2 3.0 %collective-permute-start.6 = (bf16[416,1024]{1,0:T(8,128)(2,1)}, bf16[416,1024]{1,0:T(8,128)(2,1)S(1)}, u32[]{:S(2)}, u32[]{:S(2)}) collective-permute-start(bf16[416,1024]{1,0:T(8,128)(2,1)} %bitcast.26), channel_id=1, source_target_pairs={{0,32},{1,33},{2,34},{3,35},{4,36},{5,37},{6,38},{7,39},{8,40},{9,... | collective-permute-start | bytes 2555912 | tf_op jit(solution)/shard_map/sketch_core/ppermute | solution.py:28
  127.2 1.5 %fusion.9 = f32[56,416]{1,0:T(8,128)S(1)} fusion(bf16[56,1024]{1,0:T(8,128)(2,1)S(1)} %get-tuple-element.28, bf16[416,1024]{1,0:T(8,128)(2,1)} %bitcast.26), kind=kOutput, calls=%fused_computation.44 | convolution fusion | flops 47710208 | bytes 1059840 | tf_op jit(solution)/shard_map/decode/dot_general | solution.py:116
  128.9 2.9 %fusion.2 = bf16[832,896]{1,0:T(8,128)(2,1)S(1)} fusion(bf16[832,896]{1,0:T(8,128)(2,1)S(1)} %broadcast_in_dim.8, s32[]{:T(128)S(6)} %select_n.84, bf16[416,1024]{1,0:T(8,128)(2,1)} %bitcast.26, bf16[896,512]{1,0:T(8,128)(2,1)S(1)} %bitcast.68, f32[832,896]{1,0:T(8,128)} %subtract_bitcast_fusion), kind=kOutput, calls=%fused_computation.8 | convolution fusion | flops 768151552 | bytes 4005892 | tf_op jit(solution)/shard_map/decode/dot_general | solution.py:113
  133.1 1.1 fusion.3
  134.2 1.1 copy-done.4
  (51 shorter events, 6.3 us)
Async XLA Ops:
  0.6 10.5 %copy-start.5 = (bf16[56,512]{1,0:T(8,128)(2,1)S(1)}, bf16[56,512]{1,0:T(8,128)(2,1)}, u32[]{:S(2)}) copy-start(bf16[56,512]{1,0:T(8,128)(2,1)} %param.7) | copy-start | bytes 172036
  0.6 39.6 %all-to-all-start = ((bf16[8,104,896]{2,1,0:T(8,128)(2,1)}), bf16[8,104,896]{2,1,0:T(8,128)(2,1)S(1)}, u32[]{:S(2)}, u32[]{:S(2)}) async-start(bf16[8,104,896]{2,1,0:T(8,128)(2,1)} %bitcast.76), calls=%async_computation | async-start | bytes 2981888 | tf_op jit(solution)/shard_map/local_columns/all_to_all | solution.py:72
  11.2 14.1 %collective-permute-start = (bf16[56,512]{1,0:T(8,128)(2,1)S(1)}, bf16[56,512]{1,0:T(8,128)(2,1)S(1)}, u32[]{:S(2)}, u32[]{:S(2)}) collective-permute-start(bf16[56,512]{1,0:T(8,128)(2,1)S(1)} %copy-done.5), channel_id=1, source_target_pairs={{0,256},{1,257},{2,258},{3,259},{4,260},{5,261},{6,262},{7,263},{8... | collective-permute-start | bytes 172040 | tf_op jit(solution)/shard_map/sketch_rows_zhi/ppermute | solution.py:28
  40.3 0.9 copy-start
  40.6 17.0 %copy-start.3 = (f32[56,832]{1,0:T(8,128)S(1)}, f32[56,832]{1,0:T(8,128)}, u32[]{:S(2)}) copy-start(f32[56,832]{1,0:T(8,128)} %param.6) | copy-start | bytes 559108
  57.6 16.8 %collective-permute-start.1 = (f16[56,832]{1,0:T(8,128)(2,1)S(1)}, f16[56,832]{1,0:T(8,128)(2,1)S(1)}, u32[]{:S(2)}, u32[]{:S(2)}) collective-permute-start(f16[56,832]{1,0:T(8,128)(2,1)S(1)} %multiply_convert_fusion), channel_id=1, source_target_pairs={{0,256},{1,257},{2,258},{3,259},{4,260},{5,261},{6,262},{7,263},{8... | collective-permute-start | bytes 279560 | tf_op jit(solution)/shard_map/sketch_sum/ppermute | solution.py:28
  71.2 15.3 %all-to-all-start.2 = ((f32[4,8,512]{2,1,0:T(8,128)}), f32[4,8,512]{2,1,0:T(8,128)S(1)}, u32[]{:S(2)}, u32[]{:S(2)}) async-start(f32[4,8,512]{2,1,0:T(8,128)} %broadcast_in_dim.9), calls=%async_computation.2 | async-start | bytes 131072 | tf_op jit(solution)/shard_map/sketch_sum/all_to_all | solution.py:46
  74.6 17.7 %collective-permute-start.2 = (f16[112,832]{1,0:T(8,128)(2,1)S(1)}, f16[112,832]{1,0:T(8,128)(2,1)S(1)}, u32[]{:S(2)}, u32[]{:S(2)}) collective-permute-start(f16[112,832]{1,0:T(8,128)(2,1)S(1)} %bitcast.71), channel_id=1, source_target_pairs={{0,192},{1,193},{2,194},{3,195},{4,196},{5,197},{6,198},{7,199},{8... | collective-permute-start | bytes 559112 | tf_op jit(solution)/shard_map/sketch_sum/ppermute | solution.py:36
  78.6 13.7 %collective-permute-start.3 = (f16[112,832]{1,0:T(8,128)(2,1)S(1)}, f16[112,832]{1,0:T(8,128)(2,1)S(1)}, u32[]{:S(2)}, u32[]{:S(2)}) collective-permute-start(f16[112,832]{1,0:T(8,128)(2,1)S(1)} %bitcast.72), channel_id=1, source_target_pairs={{0,128},{1,129},{2,130},{3,131},{4,132},{5,133},{6,134},{7,135},{8... | collective-permute-start | bytes 559112 | tf_op jit(solution)/shard_map/sketch_sum/ppermute | solution.py:36
  81.1 11.3 %collective-permute-start.4 = (f16[112,832]{1,0:T(8,128)(2,1)S(1)}, f16[112,832]{1,0:T(8,128)(2,1)S(1)}, u32[]{:S(2)}, u32[]{:S(2)}) collective-permute-start(f16[112,832]{1,0:T(8,128)(2,1)S(1)} %bitcast.73), channel_id=1, source_target_pairs={{0,64},{1,65},{2,66},{3,67},{4,68},{5,69},{6,70},{7,71},{8,72},{9,... | collective-permute-start | bytes 559112 | tf_op jit(solution)/shard_map/sketch_sum/ppermute | solution.py:36
  87.2 13.9 %all-to-all-start.3 = ((f32[16,8,512]{2,1,0:T(8,128)}), f32[16,8,512]{2,1,0:T(8,128)S(1)}, u32[]{:S(2)}, u32[]{:S(2)}) async-start(f32[16,8,512]{2,1,0:T(8,128)} %broadcast_in_dim.10), calls=%async_computation.3 | async-start | bytes 524288 | tf_op jit(solution)/shard_map/sketch_sum/all_to_all | solution.py:46
  102.1 9.1 %collective-permute-start.5 = (f16[4,112,832]{2,1,0:T(8,128)(2,1)S(1)}, f16[4,112,832]{2,1,0:T(8,128)(2,1)S(1)}, u32[]{:S(2)}, u32[]{:S(2)}) collective-permute-start(f16[4,112,832]{2,1,0:T(8,128)(2,1)S(1)} %constant_dynamic-slice_fusion), channel_id=1, source_target_pairs={{0,32},{1,33},{2,34},{3,35},{4,36},{5,37},{6,38},{7,39},{8,40},{9,... | collective-permute-start | bytes 2236424 | tf_op jit(solution)/shard_map/momentum_core/ppermute | solution.py:28
  107.1 17.2 %all-to-all-start.4 = ((bf16[4,104,1024]{2,1,0:T(8,128)(2,1)}), bf16[4,104,1024]{2,1,0:T(8,128)(2,1)}, u32[]{:S(2)}, u32[]{:S(2)}) async-start(bf16[4,104,1024]{2,1,0:T(8,128)(2,1)} %broadcast_in_dim.11), calls=%async_computation.4 | async-start | bytes 1703936 | tf_op jit(solution)/shard_map/sketch_y/all_to_all | solution.py:100
  119.5 9.4 %copy-start.1 = (bf16[2,8,56,512]{3,2,1,0:T(8,128)(2,1)S(1)}, bf16[2,8,56,512]{3,2,1,0:T(8,128)(2,1)}, u32[]{:S(2)}) copy-start(bf16[2,8,56,512]{3,2,1,0:T(8,128)(2,1)} %copy-done) | copy-start | bytes 2752516
  124.2 7.6 %collective-permute-start.6 = (bf16[416,1024]{1,0:T(8,128)(2,1)}, bf16[416,1024]{1,0:T(8,128)(2,1)S(1)}, u32[]{:S(2)}, u32[]{:S(2)}) collective-permute-start(bf16[416,1024]{1,0:T(8,128)(2,1)} %bitcast.26), channel_id=1, source_target_pairs={{0,32},{1,33},{2,34},{3,35},{4,36},{5,37},{6,38},{7,39},{8,40},{9,... | collective-permute-start | bytes 2555912 | tf_op jit(solution)/shard_map/sketch_core/ppermute | solution.py:28
  128.9 4.2 %copy-start.2 = (f32[832,896]{1,0:T(8,128)S(1)}, f32[832,896]{1,0:T(8,128)}, u32[]{:S(2)}) copy-start(f32[832,896]{1,0:T(8,128)} %subtract_bitcast_fusion) | copy-start | bytes 8945668
  134.2 1.1 copy-start.4
